TPU v7x, 512 devices: a whole 4x4x16 slice. The times are simulated.
512 devices in a mesh: gx: 16 (over x_hi, y, core), gy: 32 (over z, x_lo).
Axes of the slice: x: 4 (x_hi: 2, x_lo: 2; x = x_hi * 2 + x_lo), y: 4, z: 16, core: 2. Of those that a mesh axis runs over, the one named last changes fastest.
Arguments:
- phase: float32 [128, 256, 256], P('gx', 'gy'), may hold values from -1 to 1
- solute: float32 [128, 256, 256], P('gx', 'gy'), may hold values from -0.5 to 0.5
- grain: int32 [128, 256, 256], P('gx', 'gy'), may hold values from 0 to 15
- grain_angle: float32 [16], replicated, may hold values from -3.140625 to 3.140625
- inlet_flags: int32 [256, 256], P('gy', 'gx'), may hold values 0 or 1
- populations: float32 [19, 256, 256, 128], P(None, 'gy', 'gx'), may hold values from 0.4 to 1.6
Outputs:
- phase_next: float32 [128, 256, 256], P('gx', 'gy')
- solute_next: float32 [128, 256, 256], P('gx', 'gy')
- populations_next: float32 [19, 256, 256, 128], P(None, 'gy', 'gx')
All inputs are finite; a program needn't handle non-finite values. No bound on the sum of `inlet_flags` on one device may be relied on, other than what follows from the above.
Results may differ from a plain program's by a relative error of at most 0.00002.
Values sent between devices are 32-bit elements; how exact they have to be, the bound alone decides.
A program may use at most 64 MiB of HBM per device.

v0:
```python
import jax
import jax.numpy as jnp
from jax import lax
from jax.sharding import PartitionSpec as P

LB_STEPS = 2


VELOCITY = (
    (0, 0, 0),
    (1, 0, 0),
    (-1, 0, 0),
    (0, 1, 0),
    (0, -1, 0),
    (0, 0, 1),
    (0, 0, -1),
    (1, 1, 0),
    (-1, -1, 0),
    (1, -1, 0),
    (-1, 1, 0),
    (1, 0, 1),
    (-1, 0, -1),
    (1, 0, -1),
    (-1, 0, 1),
    (0, 1, 1),
    (0, -1, -1),
    (0, 1, -1),
    (0, -1, 1),
)
WEIGHTS = (1.0 / 3.0,) + (1.0 / 18.0,) * 6 + (1.0 / 36.0,) * 12
OPPOSITE = (0, 2, 1, 4, 3, 6, 5, 8, 7, 10, 9, 12, 11, 14, 13, 16, 15, 18, 17)
TIME_STEP = 0.08
DIFFUSION = 2.0
COUPLING = 1.5
ANISO_STRENGTH = 0.3
RELAX_TIME = 0.8
BODY_FORCE = 0.01


def extended(value, sides, width):
    for axis, dim in sides:
        count, length = (lax.axis_size(axis), value.shape[dim])
        up = [(i, (i + 1) % count) for i in range(count)]
        down = [(j, i) for i, j in up]
        last = lax.slice_in_dim(value, length - width, length, axis=dim)
        leading = lax.slice_in_dim(value, 0, width, axis=dim)
        before = lax.ppermute(last, axis, up)
        after = lax.ppermute(leading, axis, down)
        value = jnp.concatenate([before, value, after], axis=dim)
    return value


def collide(fields, solid):
    density = fields[0]
    mom_x = jnp.zeros_like(solid)
    mom_y = jnp.zeros_like(solid)
    mom_z = jnp.zeros_like(solid)
    for comp in range(1, 19):
        density = density + fields[comp]
    for comp in range(19):
        vel = VELOCITY[comp]
        mom_x = mom_x + vel[0] * fields[comp]
        mom_y = mom_y + vel[1] * fields[comp]
        mom_z = mom_z + vel[2] * fields[comp]
    vel_x = (mom_x + 0.5 * BODY_FORCE) / density
    vel_y = mom_y / density
    vel_z = mom_z / density
    speed_sq = vel_x * vel_x + vel_y * vel_y + vel_z * vel_z
    posts = []
    for comp in range(19):
        vel = VELOCITY[comp]
        along = vel[0] * vel_x + vel[1] * vel_y + vel[2] * vel_z
        equil = WEIGHTS[comp] * density * (1.0 + 3.0 * along + 4.5 * along * along - 1.5 * speed_sq)
        relaxed = (
            fields[comp]
            - (fields[comp] - equil) / RELAX_TIME
            + 3.0 * WEIGHTS[comp] * vel[0] * BODY_FORCE
        )
        posts.append((1.0 - solid) * relaxed + solid * fields[OPPOSITE[comp]])
    return posts


def phase_update(phase, solute, xplus, xminus, yplus, yminus, zplus, zminus, cos_cell, sin_cell):
    laplace_phase = (
        xplus[0] + xminus[0] + (yplus[0] + yminus[0]) + (zplus[0] + zminus[0]) - 6.0 * phase
    )
    laplace_solute = (
        xplus[1] + xminus[1] + (yplus[1] + yminus[1]) + (zplus[1] + zminus[1]) - 6.0 * solute
    )
    grad_x = 0.5 * (xplus[0] - xminus[0])
    grad_y = 0.5 * (yplus[0] - yminus[0])
    square_x = grad_x * grad_x
    square_y = grad_y * grad_y
    denom = square_x + square_y + 0.25
    denom = denom * denom
    cos_four = (square_x * square_x - 6.0 * square_x * square_y + square_y * square_y) / denom
    sin_four = 4.0 * grad_x * grad_y * (square_x - square_y) / denom
    aniso = 1.0 + ANISO_STRENGTH * (cos_four * cos_cell + sin_four * sin_cell)
    bulk = 1.0 - phase * phase
    phase_next = phase + TIME_STEP * aniso * aniso * (
        laplace_phase + phase - phase * phase * phase - COUPLING * solute * bulk * bulk
    )
    solute_next = solute + TIME_STEP * DIFFUSION * laplace_solute + 0.5 * (phase_next - phase)
    return (phase_next, solute_next)


def stream_whole(posts):
    cross = posts[0].shape[0]
    third = posts[0].shape[1]
    padded = extended(jnp.stack(posts), (("gx", 2), ("gy", 1)), 1)
    fields = []
    for comp in range(19):
        vel = VELOCITY[comp]
        moved = padded[comp, 1 - vel[1] : 1 - vel[1] + cross, 1 - vel[2] : 1 - vel[2] + third, :]
        fields.append(jnp.roll(moved, vel[0], -1))
    return fields


def per_device(phase, solute, grain, grain_angle, inlet_flags, populations):
    stacked = jnp.stack([phase, solute])
    padded = extended(stacked, (("gx", 1), ("gy", 2)), 1)
    xplus = padded[:, 2:, 1:-1]
    xminus = padded[:, :-2, 1:-1]
    yplus = padded[:, 1:-1, 2:]
    yminus = padded[:, 1:-1, :-2]
    zplus = jnp.roll(stacked, -1, 3)
    zminus = jnp.roll(stacked, 1, 3)
    cos_table = jnp.cos(4.0 * grain_angle)
    sin_table = jnp.sin(4.0 * grain_angle)
    cos_cell = jnp.zeros_like(phase)
    sin_cell = jnp.zeros_like(phase)
    for which in range(grain_angle.shape[0]):
        chosen = grain == which
        cos_cell = jnp.where(chosen, cos_table[which], cos_cell)
        sin_cell = jnp.where(chosen, sin_table[which], sin_cell)
    phase_next, solute_next = phase_update(
        phase, solute, xplus, xminus, yplus, yminus, zplus, zminus, cos_cell, sin_cell
    )
    solid = jnp.clip(0.5 * (1.0 + phase_next), 0.0, 1.0)
    regrouped = lax.all_to_all(solid, "gx", split_axis=2, concat_axis=0, tiled=True)
    solid_p = jnp.transpose(regrouped, (1, 2, 0))
    solid_p = solid_p.at[:, :, 0].set(jnp.where(inlet_flags == 0, 1.0, solid_p[:, :, 0]))
    fields = [populations[comp] * WEIGHTS[comp] for comp in range(19)]
    for step in range(LB_STEPS):
        posts = collide(fields, solid_p)
        fields = stream_whole(posts)
    populations_next = jnp.stack([fields[comp] / WEIGHTS[comp] for comp in range(19)])
    return (phase_next, solute_next, populations_next)


def solution(mesh):
    return jax.shard_map(
        per_device,
        mesh=mesh,
        in_specs=(
            P("gx", "gy", None),
            P("gx", "gy", None),
            P("gx", "gy", None),
            P(),
            P("gy", "gx"),
            P(None, "gy", "gx", None),
        ),
        out_specs=(P("gx", "gy", None), P("gx", "gy", None), P(None, "gy", "gx", None)),
        check_vma=False,
    )
```

profile of v0, /device:TPU:66, one launch (start us, length us, event | category | flops | bytes accessed | tf_op | source)
XLA Modules:
  0.0 122.5 jit_solution(13127474143800019748)
XLA Ops:
  0.7 0.8 pad_maximum_fusion.54
  1.5 1.9 %collective-permute-start.1 = (f32[2,1,8,256]{3,2,1,0:T(8,128)S(1)}, f32[2,1,8,256]{3,2,1,0:T(8,128)S(1)}, u32[]{:S(2)}, u32[]{:S(2)}) collective-permute-start(f32[2,1,8,256]{3,2,1,0:T(8,128)S(1)} %get-tuple-element.107), channel_id=1, source_target_pairs={{0,32},{32,64},{64,96},{96,128},{128,160},{160,192},{192,224},{224... | collective-permute-start | bytes 49160 | tf_op jit(solution)/shard_map/ppermute | solution.py:47
  3.4 7.3 %collective-permute-start = (f32[2,1,8,256]{3,2,1,0:T(8,128)S(1)}, f32[2,1,8,256]{3,2,1,0:T(8,128)S(1)}, u32[]{:S(2)}, u32[]{:S(2)}) collective-permute-start(f32[2,1,8,256]{3,2,1,0:T(8,128)S(1)} %get-tuple-element.108), channel_id=1, source_target_pairs={{32,0},{64,32},{96,64},{128,96},{160,128},{192,160},{224,192},{256... | collective-permute-start | bytes 49160 | tf_op jit(solution)/shard_map/ppermute | solution.py:48
  10.6 1.0 fusion
  11.6 0.9 fusion.369
  12.5 0.7 multiply_cosine_fusion
  13.2 1.0 fusion.1
  14.2 0.7 fusion.434
  14.9 1.0 pad_maximum_fusion.53
  15.9 3.8 %collective-permute-start.3 = (f32[2,10,1,256]{3,0,2,1:T(2,128)S(1)}, f32[2,10,1,256]{3,0,2,1:T(2,128)S(1)}, u32[]{:S(2)}, u32[]{:S(2)}) collective-permute-start(f32[2,10,1,256]{3,0,2,1:T(2,128)S(1)} %copy.1102), channel_id=1, source_target_pairs={{0,1},{1,2},{2,3},{3,4},{4,5},{5,6},{6,7},{7,8},{8,9},{9,10},{10,1... | collective-permute-start | bytes 61448 | tf_op jit(solution)/shard_map/ppermute | solution.py:47
  19.7 2.0 %collective-permute-start.2 = (f32[2,10,1,256]{3,0,2,1:T(2,128)S(1)}, f32[2,10,1,256]{3,0,2,1:T(2,128)S(1)}, u32[]{:S(2)}, u32[]{:S(2)}) collective-permute-start(f32[2,10,1,256]{3,0,2,1:T(2,128)S(1)} %copy.1101), channel_id=1, source_target_pairs={{1,0},{2,1},{3,2},{4,3},{5,4},{6,5},{7,6},{8,7},{9,8},{10,9},{11,1... | collective-permute-start | bytes 61448 | tf_op jit(solution)/shard_map/ppermute | solution.py:48
  21.8 0.7 fusion.435
  22.5 3.8 %collective-permute-done.2 = f32[2,10,1,256]{3,0,2,1:T(2,128)S(1)} collective-permute-done((f32[2,10,1,256]{3,0,2,1:T(2,128)S(1)}, f32[2,10,1,256]{3,0,2,1:T(2,128)S(1)}, u32[]{:S(2)}, u32[]{:S(2)}) %collective-permute-start.2) | collective-permute-done | bytes 20512 | tf_op jit(solution)/shard_map/ppermute | solution.py:48
  26.4 20.2 %multiply_clamp_fusion = (f32[8,8,256]{2,1,0:T(8,128)S(1)}, f32[8,8,256]{2,1,0:T(8,128)S(1)}) fusion(f32[8,8,256]{2,1,0:T(8,128)S(1)} %copy-done.1, f32[8,8,256]{2,1,0:T(8,128)S(1)} %copy-done.2, f32[2,8,8,256]{3,2,1,0:T(8,128)S(1)} %fusion.1, f32[2,8,8,1]{3,2,1,0:T(8,128)S(1)} %get-tuple-element.109, f32[2,8,8,255]{3,2,1,0:T(8,128)S(1)} %fusion, ...), kind=kLoop, calls=%fused_computation.718 | loop fusion | flops 1802240 | bytes 729216 | tf_op jit(solution)/shard_map/jit(clip)/min | solution.py:139
  46.6 0.4 copy.1067
  47.0 0.5 reshape.453
  47.5 11.3 %all_to_all.18 = f32[16,1,1024]{2,1,0:T(1,128)S(1)} all-to-all(f32[16,1,1024]{2,1,0:T(1,128)S(1)} %reshape.453), channel_id=1, replica_groups=mesh['gx'=16,'gy'=32] {'gx'}, dimensions={0} | all-to-all | bytes 131072 | tf_op jit(solution)/shard_map/all_to_all | solution.py:140
  58.8 0.5 broadcast.830
  59.3 0.8 reduce.4
  60.1 0.6 reshape.454
  60.7 0.3 copy.1068
  61.0 0.2 copy.1069
  61.2 0.1 slice_reduce_fusion
  61.4 0.1 copy.1070
  61.5 0.1 scatter.4
  61.6 0.4 copy-done
  62.0 0.3 constant_dynamic-update-slice_fusion.18
  63.5 0.1 fusion.433
  63.6 2.9 %collective-permute-start.5 = (f32[19,8,1,128]{3,1,2,0:T(8,128)S(1)}, f32[19,8,1,128]{3,1,2,0:T(8,128)S(1)}, u32[]{:S(2)}, u32[]{:S(2)}) collective-permute-start(f32[19,8,1,128]{3,1,2,0:T(8,128)S(1)} %bitcast.854), channel_id=1, source_target_pairs={{32,0},{64,32},{96,64},{128,96},{160,128},{192,160},{224,192},{256... | collective-permute-start | bytes 233480 | tf_op jit(solution)/shard_map/ppermute | solution.py:48
  66.5 1.9 %collective-permute-start.4 = (f32[19,8,1,128]{3,1,2,0:T(8,128)S(1)}, f32[19,8,1,128]{3,1,2,0:T(8,128)S(1)}, u32[]{:S(2)}, u32[]{:S(2)}) collective-permute-start(f32[19,8,1,128]{3,1,2,0:T(8,128)S(1)} %bitcast.852), channel_id=1, source_target_pairs={{0,32},{32,64},{64,96},{96,128},{128,160},{160,192},{192,224},{224... | collective-permute-start | bytes 233480 | tf_op jit(solution)/shard_map/ppermute | solution.py:47
  68.5 7.3 %collective-permute-done.4 = f32[19,8,1,128]{3,1,2,0:T(8,128)S(1)} collective-permute-done((f32[19,8,1,128]{3,1,2,0:T(8,128)S(1)}, f32[19,8,1,128]{3,1,2,0:T(8,128)S(1)}, u32[]{:S(2)}, u32[]{:S(2)}) %collective-permute-start.4) | collective-permute-done | bytes 77856 | tf_op jit(solution)/shard_map/ppermute | solution.py:47
  75.9 0.2 copy.1077
  76.1 0.2 copy.1075
  76.3 4.2 %collective-permute-start.6 = (f32[19,1,18,128]{3,1,2,0:T(1,128)S(1)}, f32[19,1,18,128]{3,1,2,0:T(1,128)S(1)}, u32[]{:S(2)}, u32[]{:S(2)}) collective-permute-start(f32[19,1,18,128]{3,1,2,0:T(1,128)S(1)} %copy.1075), channel_id=1, source_target_pairs={{0,1},{1,2},{2,3},{3,4},{4,5},{5,6},{6,7},{7,8},{8,9},{9,10},{10,1... | collective-permute-start | bytes 525320 | tf_op jit(solution)/shard_map/ppermute | solution.py:47
  80.5 1.9 %collective-permute-start.7 = (f32[19,1,18,128]{3,1,2,0:T(1,128)S(1)}, f32[19,1,18,128]{3,1,2,0:T(1,128)S(1)}, u32[]{:S(2)}, u32[]{:S(2)}) collective-permute-start(f32[19,1,18,128]{3,1,2,0:T(1,128)S(1)} %copy.1077), channel_id=1, source_target_pairs={{1,0},{2,1},{3,2},{4,3},{5,4},{6,5},{7,6},{8,7},{9,8},{10,9},{11,1... | collective-permute-start | bytes 525320 | tf_op jit(solution)/shard_map/ppermute | solution.py:48
  82.4 0.7 fusion.383
  83.5 0.1 slice.715
  83.6 0.1 slice.717
  83.7 1.4 %collective-permute-done.6 = f32[19,1,18,128]{3,1,2,0:T(1,128)S(1)} collective-permute-done((f32[19,1,18,128]{3,1,2,0:T(1,128)S(1)}, f32[19,1,18,128]{3,1,2,0:T(1,128)S(1)}, u32[]{:S(2)}, u32[]{:S(2)}) %collective-permute-start.6) | collective-permute-done | bytes 175136 | tf_op jit(solution)/shard_map/ppermute | solution.py:47
  85.1 8.0 %collective-permute-done.7 = f32[19,1,18,128]{3,1,2,0:T(1,128)S(1)} collective-permute-done((f32[19,1,18,128]{3,1,2,0:T(1,128)S(1)}, f32[19,1,18,128]{3,1,2,0:T(1,128)S(1)}, u32[]{:S(2)}, u32[]{:S(2)}) %collective-permute-start.7) | collective-permute-done | bytes 175136 | tf_op jit(solution)/shard_map/ppermute | solution.py:48
  93.3 0.1 slice.707
  93.4 0.1 slice.709
  93.5 0.5 constant_dynamic-update-slice_fusion.37
  95.2 0.1 fusion.432
  95.4 1.9 %collective-permute-start.9 = (f32[19,8,1,128]{3,1,2,0:T(8,128)S(1)}, f32[19,8,1,128]{3,1,2,0:T(8,128)S(1)}, u32[]{:S(2)}, u32[]{:S(2)}) collective-permute-start(f32[19,8,1,128]{3,1,2,0:T(8,128)S(1)} %bitcast.853), channel_id=1, source_target_pairs={{32,0},{64,32},{96,64},{128,96},{160,128},{192,160},{224,192},{256... | collective-permute-start | bytes 233480 | tf_op jit(solution)/shard_map/ppermute | solution.py:48
  97.3 2.4 %collective-permute-start.8 = (f32[19,8,1,128]{3,1,2,0:T(8,128)S(1)}, f32[19,8,1,128]{3,1,2,0:T(8,128)S(1)}, u32[]{:S(2)}, u32[]{:S(2)}) collective-permute-start(f32[19,8,1,128]{3,1,2,0:T(8,128)S(1)} %bitcast.851), channel_id=1, source_target_pairs={{0,32},{32,64},{64,96},{96,128},{128,160},{160,192},{192,224},{224... | collective-permute-start | bytes 233480 | tf_op jit(solution)/shard_map/ppermute | solution.py:47
  99.8 7.4 %collective-permute-done.8 = f32[19,8,1,128]{3,1,2,0:T(8,128)S(1)} collective-permute-done((f32[19,8,1,128]{3,1,2,0:T(8,128)S(1)}, f32[19,8,1,128]{3,1,2,0:T(8,128)S(1)}, u32[]{:S(2)}, u32[]{:S(2)}) %collective-permute-start.8) | collective-permute-done | bytes 77856 | tf_op jit(solution)/shard_map/ppermute | solution.py:47
  107.2 0.2 copy.1087
  107.4 4.2 %collective-permute-start.10 = (f32[19,1,18,128]{3,1,2,0:T(1,128)S(1)}, f32[19,1,18,128]{3,1,2,0:T(1,128)S(1)}, u32[]{:S(2)}, u32[]{:S(2)}) collective-permute-start(f32[19,1,18,128]{3,1,2,0:T(1,128)S(1)} %copy.1087), channel_id=1, source_target_pairs={{0,1},{1,2},{2,3},{3,4},{4,5},{5,6},{6,7},{7,8},{8,9},{9,10},{10,1... | collective-permute-start | bytes 525320 | tf_op jit(solution)/shard_map/ppermute | solution.py:47
  111.6 0.1 constant_dynamic-update-slice_fusion.55
  111.7 0.1 constant_dynamic-update-slice_fusion.54
  111.8 0.2 copy.1089
  112.0 1.9 %collective-permute-start.11 = (f32[19,1,18,128]{3,1,2,0:T(1,128)S(1)}, f32[19,1,18,128]{3,1,2,0:T(1,128)S(1)}, u32[]{:S(2)}, u32[]{:S(2)}) collective-permute-start(f32[19,1,18,128]{3,1,2,0:T(1,128)S(1)} %copy.1089), channel_id=1, source_target_pairs={{1,0},{2,1},{3,2},{4,3},{5,4},{6,5},{7,6},{8,7},{9,8},{10,9},{11,1... | collective-permute-start | bytes 525320 | tf_op jit(solution)/shard_map/ppermute | solution.py:48
  113.9 0.8 collective-permute-done.10
  115.3 4.9 %collective-permute-done.11 = f32[19,1,18,128]{3,1,2,0:T(1,128)S(1)} collective-permute-done((f32[19,1,18,128]{3,1,2,0:T(1,128)S(1)}, f32[19,1,18,128]{3,1,2,0:T(1,128)S(1)}, u32[]{:S(2)}, u32[]{:S(2)}) %collective-permute-start.11) | collective-permute-done | bytes 175136 | tf_op jit(solution)/shard_map/ppermute | solution.py:48
  120.6 0.1 constant_dynamic-update-slice_fusion.49
  120.7 0.1 constant_dynamic-update-slice_fusion.48
  120.8 0.1 constant_dynamic-update-slice_fusion.47
  120.9 0.1 constant_dynamic-update-slice_fusion.46
  121.0 0.1 constant_dynamic-update-slice_fusion.45
  121.1 0.1 constant_dynamic-update-slice_fusion.44
  121.1 0.1 constant_dynamic-update-slice_fusion.43
  121.2 0.1 constant_dynamic-update-slice_fusion.42
  121.4 1.0 copy-done.6
  (100 shorter events, 4.2 us)
Async XLA Ops:
  0.6 25.7 %copy-start.2 = (f32[8,8,256]{2,1,0:T(8,128)S(1)}, f32[8,8,256]{2,1,0:T(8,128)}, u32[]{:S(2)}) copy-start(f32[8,8,256]{2,1,0:T(8,128)} %param.9) | copy-start | bytes 196612
  0.6 25.7 %copy-start.1 = (f32[8,8,256]{2,1,0:T(8,128)S(1)}, f32[8,8,256]{2,1,0:T(8,128)}, u32[]{:S(2)}) copy-start(f32[8,8,256]{2,1,0:T(8,128)} %param.8) | copy-start | bytes 196612
  0.7 25.7 %copy-start.4 = (s32[8,8,256]{2,1,0:T(8,128)S(1)}, s32[8,8,256]{2,1,0:T(8,128)}, u32[]{:S(2)}) copy-start(s32[8,8,256]{2,1,0:T(8,128)} %param.10) | copy-start | bytes 196612
  1.5 13.5 %collective-permute-start.1 = (f32[2,1,8,256]{3,2,1,0:T(8,128)S(1)}, f32[2,1,8,256]{3,2,1,0:T(8,128)S(1)}, u32[]{:S(2)}, u32[]{:S(2)}) collective-permute-start(f32[2,1,8,256]{3,2,1,0:T(8,128)S(1)} %get-tuple-element.107), channel_id=1, source_target_pairs={{0,32},{32,64},{64,96},{96,128},{128,160},{160,192},{192,224},{224... | collective-permute-start | bytes 49160 | tf_op jit(solution)/shard_map/ppermute | solution.py:47
  3.4 11.5 %collective-permute-start = (f32[2,1,8,256]{3,2,1,0:T(8,128)S(1)}, f32[2,1,8,256]{3,2,1,0:T(8,128)S(1)}, u32[]{:S(2)}, u32[]{:S(2)}) collective-permute-start(f32[2,1,8,256]{3,2,1,0:T(8,128)S(1)} %get-tuple-element.108), channel_id=1, source_target_pairs={{32,0},{64,32},{96,64},{128,96},{160,128},{192,160},{224,192},{256... | collective-permute-start | bytes 49160 | tf_op jit(solution)/shard_map/ppermute | solution.py:48
  15.9 6.6 %collective-permute-start.3 = (f32[2,10,1,256]{3,0,2,1:T(2,128)S(1)}, f32[2,10,1,256]{3,0,2,1:T(2,128)S(1)}, u32[]{:S(2)}, u32[]{:S(2)}) collective-permute-start(f32[2,10,1,256]{3,0,2,1:T(2,128)S(1)} %copy.1102), channel_id=1, source_target_pairs={{0,1},{1,2},{2,3},{3,4},{4,5},{5,6},{6,7},{7,8},{8,9},{9,10},{10,1... | collective-permute-start | bytes 61448 | tf_op jit(solution)/shard_map/ppermute | solution.py:47
  19.7 6.6 %collective-permute-start.2 = (f32[2,10,1,256]{3,0,2,1:T(2,128)S(1)}, f32[2,10,1,256]{3,0,2,1:T(2,128)S(1)}, u32[]{:S(2)}, u32[]{:S(2)}) collective-permute-start(f32[2,10,1,256]{3,0,2,1:T(2,128)S(1)} %copy.1101), channel_id=1, source_target_pairs={{1,0},{2,1},{3,2},{4,3},{5,4},{6,5},{7,6},{8,7},{9,8},{10,9},{11,1... | collective-permute-start | bytes 61448 | tf_op jit(solution)/shard_map/ppermute | solution.py:48
  46.5 35.9 %copy-start.3 = (f32[8,8,256]{2,1,0:T(8,128)}, f32[8,8,256]{2,1,0:T(8,128)S(1)}, u32[]{:S(2)}) copy-start(f32[8,8,256]{2,1,0:T(8,128)S(1)} %get-tuple-element.71) | copy-start | bytes 196612
  60.7 0.7 copy-start.5
  60.7 1.3 %copy-start = (f32[19,8,16,128]{3,2,1,0:T(8,128)S(1)}, f32[19,8,16,128]{3,2,1,0:T(8,128)}, u32[]{:S(2)}) copy-start(f32[19,8,16,128]{3,2,1,0:T(8,128)} %param.13) | copy-start | bytes 3735556
  63.6 4.9 %collective-permute-start.5 = (f32[19,8,1,128]{3,1,2,0:T(8,128)S(1)}, f32[19,8,1,128]{3,1,2,0:T(8,128)S(1)}, u32[]{:S(2)}, u32[]{:S(2)}) collective-permute-start(f32[19,8,1,128]{3,1,2,0:T(8,128)S(1)} %bitcast.854), channel_id=1, source_target_pairs={{32,0},{64,32},{96,64},{128,96},{160,128},{192,160},{224,192},{256... | collective-permute-start | bytes 233480 | tf_op jit(solution)/shard_map/ppermute | solution.py:48
  66.5 9.3 %collective-permute-start.4 = (f32[19,8,1,128]{3,1,2,0:T(8,128)S(1)}, f32[19,8,1,128]{3,1,2,0:T(8,128)S(1)}, u32[]{:S(2)}, u32[]{:S(2)}) collective-permute-start(f32[19,8,1,128]{3,1,2,0:T(8,128)S(1)} %bitcast.852), channel_id=1, source_target_pairs={{0,32},{32,64},{64,96},{96,128},{128,160},{160,192},{192,224},{224... | collective-permute-start | bytes 233480 | tf_op jit(solution)/shard_map/ppermute | solution.py:47
  76.3 8.8 %collective-permute-start.6 = (f32[19,1,18,128]{3,1,2,0:T(1,128)S(1)}, f32[19,1,18,128]{3,1,2,0:T(1,128)S(1)}, u32[]{:S(2)}, u32[]{:S(2)}) collective-permute-start(f32[19,1,18,128]{3,1,2,0:T(1,128)S(1)} %copy.1075), channel_id=1, source_target_pairs={{0,1},{1,2},{2,3},{3,4},{4,5},{5,6},{6,7},{7,8},{8,9},{9,10},{10,1... | collective-permute-start | bytes 525320 | tf_op jit(solution)/shard_map/ppermute | solution.py:47
  80.5 12.6 %collective-permute-start.7 = (f32[19,1,18,128]{3,1,2,0:T(1,128)S(1)}, f32[19,1,18,128]{3,1,2,0:T(1,128)S(1)}, u32[]{:S(2)}, u32[]{:S(2)}) collective-permute-start(f32[19,1,18,128]{3,1,2,0:T(1,128)S(1)} %copy.1077), channel_id=1, source_target_pairs={{1,0},{2,1},{3,2},{4,3},{5,4},{6,5},{7,6},{8,7},{9,8},{10,9},{11,1... | collective-permute-start | bytes 525320 | tf_op jit(solution)/shard_map/ppermute | solution.py:48
  95.4 4.4 %collective-permute-start.9 = (f32[19,8,1,128]{3,1,2,0:T(8,128)S(1)}, f32[19,8,1,128]{3,1,2,0:T(8,128)S(1)}, u32[]{:S(2)}, u32[]{:S(2)}) collective-permute-start(f32[19,8,1,128]{3,1,2,0:T(8,128)S(1)} %bitcast.853), channel_id=1, source_target_pairs={{32,0},{64,32},{96,64},{128,96},{160,128},{192,160},{224,192},{256... | collective-permute-start | bytes 233480 | tf_op jit(solution)/shard_map/ppermute | solution.py:48
  97.3 9.9 %collective-permute-start.8 = (f32[19,8,1,128]{3,1,2,0:T(8,128)S(1)}, f32[19,8,1,128]{3,1,2,0:T(8,128)S(1)}, u32[]{:S(2)}, u32[]{:S(2)}) collective-permute-start(f32[19,8,1,128]{3,1,2,0:T(8,128)S(1)} %bitcast.851), channel_id=1, source_target_pairs={{0,32},{32,64},{64,96},{96,128},{128,160},{160,192},{192,224},{224... | collective-permute-start | bytes 233480 | tf_op jit(solution)/shard_map/ppermute | solution.py:47
  107.4 7.3 %collective-permute-start.10 = (f32[19,1,18,128]{3,1,2,0:T(1,128)S(1)}, f32[19,1,18,128]{3,1,2,0:T(1,128)S(1)}, u32[]{:S(2)}, u32[]{:S(2)}) collective-permute-start(f32[19,1,18,128]{3,1,2,0:T(1,128)S(1)} %copy.1087), channel_id=1, source_target_pairs={{0,1},{1,2},{2,3},{3,4},{4,5},{5,6},{6,7},{7,8},{8,9},{9,10},{10,1... | collective-permute-start | bytes 525320 | tf_op jit(solution)/shard_map/ppermute | solution.py:47
  112.0 8.2 %collective-permute-start.11 = (f32[19,1,18,128]{3,1,2,0:T(1,128)S(1)}, f32[19,1,18,128]{3,1,2,0:T(1,128)S(1)}, u32[]{:S(2)}, u32[]{:S(2)}) collective-permute-start(f32[19,1,18,128]{3,1,2,0:T(1,128)S(1)} %copy.1089), channel_id=1, source_target_pairs={{1,0},{2,1},{3,2},{4,3},{5,4},{6,5},{7,6},{8,7},{9,8},{10,9},{11,1... | collective-permute-start | bytes 525320 | tf_op jit(solution)/shard_map/ppermute | solution.py:48
  121.4 1.0 copy-start.6
where the time goes:
time: 124 us; the launch traced here: 122 us
  starting transfers between devices  36.4 us (29%)
  waiting for transfers between devices  33.7 us (27%)
  other arithmetic  31.3 us (25%)
  blocking collectives  11.3 us (9%)
  local copies, waits for them, and re-layouts  8.53 us (7%)
  between operations  1.38 us (1%)
    min x1, other arithmetic, per_device(): solid = jnp.clip(0.5 * (1.0 + phase_next), 0.0, 1.0)  20.2 us
    ppermute x6, starting transfers between devices, extended(): before = lax.ppermute(last, axis, up)  18.4 us
    ppermute x6, starting transfers between devices, extended(): after = lax.ppermute(leading, axis, down)  17.9 us
    ppermute x6, waiting for transfers between devices, extended(): before = lax.ppermute(last, axis, up)  16.9 us
    ppermute x6, waiting for transfers between devices, extended(): after = lax.ppermute(leading, axis, down)  16.8 us
    all_to_all x1, blocking collectives, per_device(): lax.all_to_all(solid, 'gx', split_axis=2, concat_axis=0, tiled=True)  11.3 us
    unnamed x51, other arithmetic  3.82 us
    unnamed x18, local copies, waits for them, and re-layouts  2.59 us
  transfers between devices with their start and end apart: 12, of which 8 were waited for; matrix products, arithmetic and copies ran while one was open for 6% of the time, Pallas kernels for 0%

commit v1 on v0

v1 whole, which is shorter than its diff:
```python
import functools

import jax
import jax.numpy as jnp
from jax import lax
from jax.experimental import pallas as pl
from jax.experimental.pallas import tpu as pltpu
from jax.sharding import PartitionSpec as P

MESH = pl.DeviceIdType.MESH
VELOCITY = (
    (0, 0, 0),
    (1, 0, 0),
    (-1, 0, 0),
    (0, 1, 0),
    (0, -1, 0),
    (0, 0, 1),
    (0, 0, -1),
    (1, 1, 0),
    (-1, -1, 0),
    (1, -1, 0),
    (-1, 1, 0),
    (1, 0, 1),
    (-1, 0, -1),
    (1, 0, -1),
    (-1, 0, 1),
    (0, 1, 1),
    (0, -1, -1),
    (0, 1, -1),
    (0, -1, 1),
)
YP = (3, 7, 10, 15, 17)
YM = (4, 8, 9, 16, 18)
ZP = (5, 11, 14, 15, 18)
ZM = (6, 12, 13, 16, 17)
ORDER = YP + YM + (0, 1, 2, 5, 6, 11, 12, 13, 14)
SLOT = tuple(ORDER.index(comp) for comp in range(19))
EDGES = ((15, 1, 1), (16, -1, -1), (17, -1, 1), (18, 1, -1))
BODY_FORCE = 0.01
GRAINS = 16


def swap_groups(values, axis, size):
    values = list(values)
    length = values[0].shape[axis]
    group = lax.broadcasted_iota(jnp.int32, values[0].shape, axis) // size
    for bit in (1, 2, 4):
        upper = (group & bit) != 0
        for i in range(8):
            if i & bit == 0:
                low, high = values[i], values[i + bit]
                values[i] = jnp.where(upper, pltpu.roll(high, size * bit, axis), low)
                values[i + bit] = jnp.where(upper, high, pltpu.roll(low, length - size * bit, axis))
    return values


def collide(g, solid):
    dif = {i: g[i] - g[i + 1] for i in range(1, 19, 2)}
    add = {i: g[i] + g[i + 1] for i in range(1, 19, 2)}
    axes = add[1] + add[3] + add[5]
    diag = (add[7] + add[9]) + (add[11] + add[13]) + (add[15] + add[17])
    dens = 12.0 * g[0] + 2.0 * axes + diag
    mom_x = 2.0 * dif[1] + ((dif[7] + dif[9]) + (dif[11] + dif[13]))
    mom_y = 2.0 * dif[3] + ((dif[7] - dif[9]) + (dif[15] + dif[17]))
    mom_z = 2.0 * dif[5] + ((dif[11] - dif[13]) + (dif[15] - dif[17]))
    inv = 1.0 / dens
    ux = (mom_x + 18.0 * BODY_FORCE) * inv
    uy = mom_y * inv
    uz = mom_z * inv
    scaled = dens * (1.25 / 36.0)
    base = scaled * (1.0 - 1.5 * (ux * ux + uy * uy + uz * uz))
    square = 4.5 * scaled
    linear = 3.0 * scaled
    along = {
        1: ux,
        3: uy,
        5: uz,
        7: ux + uy,
        9: ux - uy,
        11: ux + uz,
        13: ux - uz,
        15: uy + uz,
        17: uy - uz,
    }
    posts = [None] * 19
    relaxed = base - 0.25 * g[0]
    posts[0] = relaxed + solid * (g[0] - relaxed)
    for i, a in along.items():
        even = base + square * (a * a)
        odd = linear * a
        if VELOCITY[i][0]:
            odd = odd + 3.0 * BODY_FORCE
        plus = even + odd - 0.25 * g[i]
        minus = even - odd - 0.25 * g[i + 1]
        posts[i] = plus + solid * (g[i + 1] - plus)
        posts[i + 1] = minus + solid * (g[i] - minus)
    return posts


def streamed(buf, comp, y):
    vx, vy, vz = VELOCITY[comp]
    value = buf[SLOT[comp], y + 1 - vy, 8 - vz : 24 - vz, :]
    if vx:
        value = pltpu.roll(value, vx % 128, 1)
    return value


def kernel(
    ngx, ngy,
    angle, phase, solute, grain, flags, pops,
    phase_out, solute_out, out,
    pv, ysend, yrecv, xrecv, tsend, trecv, solid_p, s1, s2, zsend, zrecv, csend, crecv,
    pop_sem, fs_sem, fr_sem, ts_sem, tr_sem, ls_sem, lr_sem,
):
    me_x, me_y = lax.axis_index("gx"), lax.axis_index("gy")

    def dev(dx, dy):
        return {"gx": lax.rem(me_x + dx + ngx, ngx), "gy": lax.rem(me_y + dy + ngy, ngy)}

    def remote(src, dst, send, recv, device):
        copy = pltpu.make_async_remote_copy(
            src_ref=src, dst_ref=dst, send_sem=send, recv_sem=recv, device_id=device, device_id_type=MESH
        )
        copy.start()
        return copy

    partners = [dev(d, 0) for d in range(1, ngx)] + [dev(0, 1), dev(0, -1)]
    partners += [dev(dx, dy) for _, dx, dy in EDGES]
    barrier = pltpu.get_barrier_semaphore()
    for device in partners:
        pl.semaphore_signal(barrier, inc=1, device_id=device, device_id_type=MESH)
    pop_copy = pltpu.make_async_copy(pops, pv, pop_sem)
    pop_copy.start()
    for field, ref in enumerate((phase, solute)):
        ysend[0, field] = ref[:, 7, :]
        ysend[1, field] = ref[:, 0, :]
    pl.semaphore_wait(barrier, len(partners))

    faces = []
    for side, step in ((0, 1), (1, -1)):
        faces.append(remote(ysend.at[side], yrecv.at[side], fs_sem.at[side], fr_sem.at[side], dev(0, step)))
    for side, step, layer in ((0, 1, 7), (1, -1, 0)):
        for field, ref in enumerate((phase, solute)):
            n = 2 + 2 * side + field
            faces.append(remote(ref.at[layer], xrecv.at[side, field], fs_sem.at[n], fr_sem.at[n], dev(step, 0)))

    lane = lax.broadcasted_iota(jnp.int32, (8, 128), 1)
    table = jnp.zeros((8, 128), jnp.float32)
    for which in range(GRAINS):
        table = jnp.where(lane == which, angle[which], table)
    cos_table, sin_table = jnp.cos(4.0 * table), jnp.sin(4.0 * table)
    cos_of = [jnp.broadcast_to(cos_table[:, i : i + 1], (8, 256)) for i in range(GRAINS)]
    sin_of = [jnp.broadcast_to(sin_table[:, i : i + 1], (8, 256)) for i in range(GRAINS)]
    cos_cell, sin_cell = [], []
    for x in range(8):
        ids = grain[x]
        c, s = cos_of, sin_of
        for bit in (1, 2, 4, 8):
            on = (ids & bit) != 0
            c = [jnp.where(on, c[2 * i + 1], c[2 * i]) for i in range(len(c) // 2)]
            s = [jnp.where(on, s[2 * i + 1], s[2 * i]) for i in range(len(s) // 2)]
        cos_cell.append(c[0])
        sin_cell.append(s[0])

    open_row = jnp.concatenate([flags[y : y + 1, :] for y in range(8)], axis=1)

    for copy in faces:
        copy.wait_recv()
    row = lax.broadcasted_iota(jnp.int32, (8, 256), 0)

    def around(ref, field, x):
        value = ref[x]
        xplus = ref[x + 1] if x < 7 else xrecv[1, field]
        xminus = ref[x - 1] if x > 0 else xrecv[0, field]
        yplus = jnp.where(row == 7, yrecv[1, field, x : x + 1, :], pltpu.roll(value, 7, 0))
        yminus = jnp.where(row == 0, yrecv[0, field, x : x + 1, :], pltpu.roll(value, 1, 0))
        zplus, zminus = pltpu.roll(value, 255, 1), pltpu.roll(value, 1, 1)
        laplace = (xplus + xminus) + (yplus + yminus) + (zplus + zminus) - 6.0 * value
        return value, laplace, xplus - xminus, yplus - yminus

    solids = []
    for x in range(8):
        ph, lap, dx, dy = around(phase, 0, x)
        so, lap_so, _, _ = around(solute, 1, x)
        gx, gy = 0.5 * dx, 0.5 * dy
        sx, sy = gx * gx, gy * gy
        denom = sx + sy + 0.25
        inv = 1.0 / (denom * denom)
        cos_four = (sx * sx - 6.0 * sx * sy + sy * sy) * inv
        sin_four = 4.0 * gx * gy * (sx - sy) * inv
        aniso = 1.0 + 0.3 * (cos_four * cos_cell[x] + sin_four * sin_cell[x])
        bulk = 1.0 - ph * ph
        change = 0.08 * aniso * aniso * (lap + ph - ph * ph * ph - 1.5 * so * bulk * bulk)
        ph_next = ph + change
        phase_out[x] = ph_next
        solute_out[x] = so + 0.16 * lap_so + 0.5 * (ph_next - ph)
        solids.append(jnp.clip(0.5 * (1.0 + ph_next), 0.0, 1.0))

    rows = swap_groups(solids, 0, 1)
    for half in range(2):
        tiles = swap_groups([r[:, 128 * half : 128 * half + 128] for r in rows], 1, 16)
        for j in range(8):
            tsend[8 * half + j] = tiles[j]
    moves = []
    for d in range(1, ngx):
        device = dev(d, 0)
        moves.append(
            remote(tsend.at[device["gx"]], trecv.at[me_x], ts_sem.at[d - 1], tr_sem.at[d - 1], device)
        )
    trecv[me_x] = tsend[me_x]
    pop_copy.wait()
    for copy in moves:
        copy.wait_recv()
    whole = trecv[...].reshape(128, 128)
    first = lax.broadcasted_iota(jnp.int32, (128, 128), 0) == 0
    whole = jnp.where(first & (open_row == 0), 1.0, whole)
    solid_p[...] = jnp.transpose(whole).reshape(8, 16, 128)

    pending = []

    def step(which, buf, source):
        def one(t, carry):
            y = lax.rem(t + 7, 8)
            posts = collide(source(y), solid_p[y])
            for comp in range(19):
                buf[SLOT[comp], y + 1, 8:24, :] = posts[comp]
            return carry

        sems = lambda n: (ls_sem.at[which, n], lr_sem.at[which, n])
        lax.fori_loop(0, 2, one, 0)
        copies = [
            remote(buf.at[0:5, 8, 8:24], buf.at[0:5, 0, 8:24], *sems(0), dev(0, 1)),
            remote(buf.at[5:10, 1, 8:24], buf.at[5:10, 9, 8:24], *sems(1), dev(0, -1)),
        ]
        for n, (comp, dx, dy) in enumerate(EDGES):
            y, z = (8 if dy > 0 else 1), (23 if dx > 0 else 8)
            csend[which, n, 0:1] = buf[SLOT[comp], y, z : z + 1, :]
            copies.append(remote(csend.at[which, n], crecv.at[which, n], *sems(2 + n), dev(dx, dy)))
        lax.fori_loop(2, 8, one, 0)
        for side, comps, z, dx in ((0, ZP, 23, 1), (1, ZM, 8, -1)):
            for n, comp in enumerate(comps):
                zsend[which, side, n] = buf[SLOT[comp], 1:9, z, :]
            copies.append(remote(zsend.at[which, side], zrecv.at[which, side], *sems(6 + side), dev(dx, 0)))
        for copy in copies:
            copy.wait_recv()
        pending.extend(copies)
        for side, comps, z in ((0, ZP, 7), (1, ZM, 24)):
            for n, comp in enumerate(comps):
                buf[SLOT[comp], 1:9, z, :] = zrecv[which, side, n]
        for n, (comp, dx, dy) in enumerate(EDGES):
            y, z = (0 if dy > 0 else 9), (7 if dx > 0 else 24)
            buf[SLOT[comp], y, z : z + 1, :] = crecv[which, n, 0:1]

    step(0, s1, lambda y: [pv[comp, y] for comp in range(19)])
    step(1, s2, lambda y: [streamed(s1, comp, y) for comp in range(19)])

    def last(y, carry):
        for comp in range(19):
            out[comp, y] = streamed(s2, comp, y)
        return carry

    lax.fori_loop(0, 8, last, 0)
    for copy in faces + moves + pending:
        copy.wait_send()


def per_device(ngx, ngy, phase, solute, grain, grain_angle, inlet_flags, populations):
    vmem = pl.BlockSpec(memory_space=pltpu.VMEM)
    return pl.pallas_call(
        functools.partial(kernel, ngx, ngy),
        out_shape=[
            jax.ShapeDtypeStruct(phase.shape, jnp.float32),
            jax.ShapeDtypeStruct(solute.shape, jnp.float32),
            jax.ShapeDtypeStruct(populations.shape, jnp.float32),
        ],
        in_specs=[pl.BlockSpec(memory_space=pltpu.SMEM), vmem, vmem, vmem, vmem, pl.BlockSpec(memory_space=pl.ANY)],
        out_specs=[vmem, vmem, vmem],
        scratch_shapes=[
            pltpu.VMEM((19, 8, 16, 128), jnp.float32),
            pltpu.VMEM((2, 2, 8, 256), jnp.float32),
            pltpu.VMEM((2, 2, 8, 256), jnp.float32),
            pltpu.VMEM((2, 2, 8, 256), jnp.float32),
            pltpu.VMEM((ngx, 8, 128), jnp.float32),
            pltpu.VMEM((ngx, 8, 128), jnp.float32),
            pltpu.VMEM((8, 16, 128), jnp.float32),
            pltpu.VMEM((19, 10, 32, 128), jnp.float32),
            pltpu.VMEM((19, 10, 32, 128), jnp.float32),
            pltpu.VMEM((2, 2, 5, 8, 128), jnp.float32),
            pltpu.VMEM((2, 2, 5, 8, 128), jnp.float32),
            pltpu.VMEM((2, 4, 8, 128), jnp.float32),
            pltpu.VMEM((2, 4, 8, 128), jnp.float32),
            pltpu.SemaphoreType.DMA,
            pltpu.SemaphoreType.DMA((6,)),
            pltpu.SemaphoreType.DMA((6,)),
            pltpu.SemaphoreType.DMA((ngx - 1,)),
            pltpu.SemaphoreType.DMA((ngx - 1,)),
            pltpu.SemaphoreType.DMA((2, 8)),
            pltpu.SemaphoreType.DMA((2, 8)),
        ],
        compiler_params=pltpu.CompilerParams(
            collective_id=0, has_side_effects=True, vmem_limit_bytes=40 * 1024 * 1024
        ),
    )(grain_angle, phase, solute, grain, inlet_flags, populations)


def solution(mesh):
    return jax.shard_map(
        functools.partial(per_device, mesh.shape["gx"], mesh.shape["gy"]),
        mesh=mesh,
        in_specs=(
            P("gx", "gy", None),
            P("gx", "gy", None),
            P("gx", "gy", None),
            P(),
            P("gy", "gx"),
            P(None, "gy", "gx", None),
        ),
        out_specs=(P("gx", "gy", None), P("gx", "gy", None), P(None, "gy", "gx", None)),
        check_vma=False,
    )
```

time: 124 us -> 45.4 us (0.37)
  the two profiles are of different devices: /device:TPU:66 before, /device:TPU:1 now
where the time goes in v1:
time: 45.4 us; the launch traced here: 45 us
  Pallas kernels  36.9 us (81%)
  local copies, waits for them, and re-layouts  7.44 us (16%)
  between operations  0.65 us (1%)
    pallas_call x1, Pallas kernels, per_device(): pl.pallas_call(functools.partial(kernel, ngx, ngy), out_shape=[jax.ShapeD...  36.9 us
    unnamed x15, local copies, waits for them, and re-layouts  7.44 us

profile of v1, /device:TPU:1, one launch (start us, length us, event | category | flops | bytes accessed | tf_op | source)
XLA Modules:
  0.0 45.0 jit_solution(14785774263380926819)
XLA Ops:
  0.6 0.0 copy-start
  0.6 1.3 %copy-done = f32[19,8,16,128]{3,2,1,0:T(8,128)S(1)} copy-done((f32[19,8,16,128]{3,2,1,0:T(8,128)S(1)}, f32[19,8,16,128]{3,2,1,0:T(8,128)}, u32[]{:S(2)}) %copy-start) | copy-done | bytes 1245208
  1.9 0.0 copy-start.1
  1.9 0.8 %copy-done.1 = f32[8,8,256]{2,1,0:T(8,128)S(1)} copy-done((f32[8,8,256]{2,1,0:T(8,128)S(1)}, f32[8,8,256]{2,1,0:T(8,128)}, u32[]{:S(2)}) %copy-start.1) | copy-done | bytes 65560
  2.8 0.0 copy-start.2
  2.8 0.8 %copy-done.2 = f32[8,8,256]{2,1,0:T(8,128)S(1)} copy-done((f32[8,8,256]{2,1,0:T(8,128)S(1)}, f32[8,8,256]{2,1,0:T(8,128)}, u32[]{:S(2)}) %copy-start.2) | copy-done | bytes 65560
  3.6 0.0 copy-start.3
  3.6 0.8 %copy-done.3 = s32[8,8,256]{2,1,0:T(8,128)S(1)} copy-done((s32[8,8,256]{2,1,0:T(8,128)S(1)}, s32[8,8,256]{2,1,0:T(8,128)}, u32[]{:S(2)}) %copy-start.3) | copy-done | bytes 65560
  4.4 0.0 copy-start.4
  4.4 0.7 %copy-done.4 = s32[8,16]{1,0:T(8,128)S(1)} copy-done((s32[8,16]{1,0:T(8,128)S(1)}, s32[8,16]{1,0:T(8,128)}, u32[]{:S(2)}) %copy-start.4) | copy-done | bytes 536
  5.1 0.0 copy-start.5
  5.1 0.7 %copy-done.5 = f32[16]{0:T(128)S(1)} copy-done((f32[16]{0:T(128)S(1)}, f32[16]{0:T(128)}, u32[]{:S(2)}) %copy-start.5) | copy-done | bytes 88
  5.8 36.9 %shard_map.85 = (f32[8,8,256]{2,1,0:T(8,128)S(1)}, f32[8,8,256]{2,1,0:T(8,128)S(1)}, f32[19,8,16,128]{3,2,1,0:T(8,128)S(1)}) custom-call(f32[16]{0:T(128)S(1)} %copy-done.5, f32[8,8,256]{2,1,0:T(8,128)S(1)} %copy-done.1, f32[8,8,256]{2,1,0:T(8,128)S(1)} %copy-done.2, s32[8,8,256]{2,1,0:T(8,128)S(1)} %copy-done.3, s32[8,16]{1,0:T(8,128)S(1)} %copy-done.4, ...), custom_call_target="tpu_custom_call" | custom-call | tf_op jit(solution)/shard_map/pallas_call | solution.py:269
  42.7 0.6 %copy.12 = f32[8,8,256]{2,1,0:T(8,128)} copy(f32[8,8,256]{2,1,0:T(8,128)S(1)} %get-tuple-element.6) | data formatting | bytes 131072
  43.4 0.6 %copy.13 = f32[8,8,256]{2,1,0:T(8,128)} copy(f32[8,8,256]{2,1,0:T(8,128)S(1)} %get-tuple-element.7) | data formatting | bytes 131072
  44.0 1.0 %copy.14 = f32[19,8,16,128]{3,2,1,0:T(8,128)} copy(f32[19,8,16,128]{3,2,1,0:T(8,128)S(1)} %get-tuple-element.8) | data formatting | bytes 2490368
Async XLA Ops:
  0.6 1.3 %copy-start = (f32[19,8,16,128]{3,2,1,0:T(8,128)S(1)}, f32[19,8,16,128]{3,2,1,0:T(8,128)}, u32[]{:S(2)}) copy-start(f32[19,8,16,128]{3,2,1,0:T(8,128)} %pops.1) | copy-start | bytes 3735556
  1.9 0.8 %copy-start.1 = (f32[8,8,256]{2,1,0:T(8,128)S(1)}, f32[8,8,256]{2,1,0:T(8,128)}, u32[]{:S(2)}) copy-start(f32[8,8,256]{2,1,0:T(8,128)} %phase.1) | copy-start | bytes 196612
  2.8 0.8 %copy-start.2 = (f32[8,8,256]{2,1,0:T(8,128)S(1)}, f32[8,8,256]{2,1,0:T(8,128)}, u32[]{:S(2)}) copy-start(f32[8,8,256]{2,1,0:T(8,128)} %solute.1) | copy-start | bytes 196612
  3.6 0.8 %copy-start.3 = (s32[8,8,256]{2,1,0:T(8,128)S(1)}, s32[8,8,256]{2,1,0:T(8,128)}, u32[]{:S(2)}) copy-start(s32[8,8,256]{2,1,0:T(8,128)} %grain.1) | copy-start | bytes 196612
  4.4 0.7 %copy-start.4 = (s32[8,16]{1,0:T(8,128)S(1)}, s32[8,16]{1,0:T(8,128)}, u32[]{:S(2)}) copy-start(s32[8,16]{1,0:T(8,128)} %flags.1) | copy-start | bytes 1540
  5.1 0.7 %copy-start.5 = (f32[16]{0:T(128)S(1)}, f32[16]{0:T(128)}, u32[]{:S(2)}) copy-start(f32[16]{0:T(128)} %angle.1) | copy-start | bytes 196

commit v2 on v1

--- a/solution.py
+++ b/solution.py
@@ -107,10 +107,10 @@
 
 def kernel(
     ngx, ngy,
-    angle, phase, solute, grain, flags, pops,
-    phase_out, solute_out, out,
-    pv, ysend, yrecv, xrecv, tsend, trecv, solid_p, s1, s2, zsend, zrecv, csend, crecv,
-    pop_sem, fs_sem, fr_sem, ts_sem, tr_sem, ls_sem, lr_sem,
+    angle_in, phase_in, solute_in, grain_in, flags_in, pops,
+    phase_out, solute_out, s2,
+    angle, phase, solute, grain, flags, pv, ysend, yrecv, xrecv, tsend, trecv, solid_p, s1, zsend, zrecv, csend, crecv,
+    in_sem, fs_sem, fr_sem, ts_sem, tr_sem, ls_sem, lr_sem,
 ):
     me_x, me_y = lax.axis_index("gx"), lax.axis_index("gy")
 
@@ -124,13 +124,19 @@
         copy.start()
         return copy
 
+    loads = []
+    for n, (src, dst) in enumerate(
+        ((phase_in, phase), (solute_in, solute), (angle_in, angle), (grain_in, grain), (flags_in, flags), (pops, pv))
+    ):
+        loads.append(pltpu.make_async_copy(src, dst, in_sem.at[n]))
+        loads[-1].start()
     partners = [dev(d, 0) for d in range(1, ngx)] + [dev(0, 1), dev(0, -1)]
     partners += [dev(dx, dy) for _, dx, dy in EDGES]
     barrier = pltpu.get_barrier_semaphore()
     for device in partners:
         pl.semaphore_signal(barrier, inc=1, device_id=device, device_id_type=MESH)
-    pop_copy = pltpu.make_async_copy(pops, pv, pop_sem)
-    pop_copy.start()
+    loads[0].wait()
+    loads[1].wait()
     for field, ref in enumerate((phase, solute)):
         ysend[0, field] = ref[:, 7, :]
         ysend[1, field] = ref[:, 0, :]
@@ -144,6 +150,7 @@
             n = 2 + 2 * side + field
             faces.append(remote(ref.at[layer], xrecv.at[side, field], fs_sem.at[n], fr_sem.at[n], dev(step, 0)))
 
+    loads[2].wait()
     lane = lax.broadcasted_iota(jnp.int32, (8, 128), 1)
     table = jnp.zeros((8, 128), jnp.float32)
     for which in range(GRAINS):
@@ -152,6 +159,7 @@
     cos_of = [jnp.broadcast_to(cos_table[:, i : i + 1], (8, 256)) for i in range(GRAINS)]
     sin_of = [jnp.broadcast_to(sin_table[:, i : i + 1], (8, 256)) for i in range(GRAINS)]
     cos_cell, sin_cell = [], []
+    loads[3].wait()
     for x in range(8):
         ids = grain[x]
         c, s = cos_of, sin_of
@@ -162,6 +170,7 @@
         cos_cell.append(c[0])
         sin_cell.append(s[0])
 
+    loads[4].wait()
     open_row = jnp.concatenate([flags[y : y + 1, :] for y in range(8)], axis=1)
 
     for copy in faces:
@@ -208,7 +217,7 @@
             remote(tsend.at[device["gx"]], trecv.at[me_x], ts_sem.at[d - 1], tr_sem.at[d - 1], device)
         )
     trecv[me_x] = tsend[me_x]
-    pop_copy.wait()
+    loads[5].wait()
     for copy in moves:
         copy.wait_recv()
     whole = trecv[...].reshape(128, 128)
@@ -254,28 +263,45 @@
     step(0, s1, lambda y: [pv[comp, y] for comp in range(19)])
     step(1, s2, lambda y: [streamed(s1, comp, y) for comp in range(19)])
 
-    def last(y, carry):
-        for comp in range(19):
-            out[comp, y] = streamed(s2, comp, y)
-        return carry
-
-    lax.fori_loop(0, 8, last, 0)
     for copy in faces + moves + pending:
         copy.wait_send()
 
 
+def finish(phase_next, solute_next, s2, phase_out, solute_out, out, buf, sems):
+    copies = [
+        pltpu.make_async_copy(phase_next, phase_out, sems.at[8]),
+        pltpu.make_async_copy(solute_next, solute_out, sems.at[9]),
+    ]
+    for copy in copies:
+        copy.start()
+    for y in range(8):
+        for comp in range(19):
+            buf[comp, y] = streamed(s2, comp, y)
+        copies.append(pltpu.make_async_copy(buf.at[:, y], out.at[:, y], sems.at[y]))
+        copies[-1].start()
+    for copy in copies:
+        copy.wait()
+
+
 def per_device(ngx, ngy, phase, solute, grain, grain_angle, inlet_flags, populations):
     vmem = pl.BlockSpec(memory_space=pltpu.VMEM)
-    return pl.pallas_call(
+    operands = (grain_angle, phase, solute, grain, inlet_flags, populations)
+    hbm = pl.BlockSpec(memory_space=pltpu.HBM)
+    phase_next, solute_next, s2 = pl.pallas_call(
         functools.partial(kernel, ngx, ngy),
         out_shape=[
             jax.ShapeDtypeStruct(phase.shape, jnp.float32),
             jax.ShapeDtypeStruct(solute.shape, jnp.float32),
-            jax.ShapeDtypeStruct(populations.shape, jnp.float32),
+            jax.ShapeDtypeStruct((19, 10, 32, 128), jnp.float32),
         ],
-        in_specs=[pl.BlockSpec(memory_space=pltpu.SMEM), vmem, vmem, vmem, vmem, pl.BlockSpec(memory_space=pl.ANY)],
+        in_specs=[hbm] * 6,
         out_specs=[vmem, vmem, vmem],
         scratch_shapes=[
+            pltpu.SMEM((16,), jnp.float32),
+            pltpu.VMEM((8, 8, 256), jnp.float32),
+            pltpu.VMEM((8, 8, 256), jnp.float32),
+            pltpu.VMEM((8, 8, 256), jnp.int32),
+            pltpu.VMEM((8, 16), jnp.int32),
             pltpu.VMEM((19, 8, 16, 128), jnp.float32),
             pltpu.VMEM((2, 2, 8, 256), jnp.float32),
             pltpu.VMEM((2, 2, 8, 256), jnp.float32),
@@ -284,12 +310,11 @@
             pltpu.VMEM((ngx, 8, 128), jnp.float32),
             pltpu.VMEM((8, 16, 128), jnp.float32),
             pltpu.VMEM((19, 10, 32, 128), jnp.float32),
-            pltpu.VMEM((19, 10, 32, 128), jnp.float32),
             pltpu.VMEM((2, 2, 5, 8, 128), jnp.float32),
             pltpu.VMEM((2, 2, 5, 8, 128), jnp.float32),
             pltpu.VMEM((2, 4, 8, 128), jnp.float32),
             pltpu.VMEM((2, 4, 8, 128), jnp.float32),
-            pltpu.SemaphoreType.DMA,
+            pltpu.SemaphoreType.DMA((6,)),
             pltpu.SemaphoreType.DMA((6,)),
             pltpu.SemaphoreType.DMA((6,)),
             pltpu.SemaphoreType.DMA((ngx - 1,)),
@@ -300,7 +325,19 @@
         compiler_params=pltpu.CompilerParams(
             collective_id=0, has_side_effects=True, vmem_limit_bytes=40 * 1024 * 1024
         ),
-    )(grain_angle, phase, solute, grain, inlet_flags, populations)
+    )(*[pltpu.with_memory_space_constraint(a, pltpu.HBM) for a in operands])
+    return pl.pallas_call(
+        finish,
+        out_shape=[
+            jax.ShapeDtypeStruct(phase.shape, jnp.float32),
+            jax.ShapeDtypeStruct(solute.shape, jnp.float32),
+            jax.ShapeDtypeStruct(populations.shape, jnp.float32),
+        ],
+        in_specs=[vmem] * 3,
+        out_specs=[hbm] * 3,
+        scratch_shapes=[pltpu.VMEM((19, 8, 16, 128), jnp.float32), pltpu.SemaphoreType.DMA((10,))],
+        compiler_params=pltpu.CompilerParams(vmem_limit_bytes=40 * 1024 * 1024),
+    )(phase_next, solute_next, s2)
 
 
 def solution(mesh):

time: 45.4 us -> 37.7 us (0.83)
  local copies, waits for them, and re-layouts: 7.44 us -> 0 us
    unnamed x15 -> x0, local copies, waits for them, and re-layouts: 7.44 us -> none
    pallas_call x1, Pallas kernels: 36.9 us -> 35.7 us  [per_device(): pl.pallas_call(functools.partial(kernel, ngx, ngy), out_shape=[jax.ShapeD...]
    pallas_call x0 -> x1, Pallas kernels: none -> 1.2 us  [per_device(): pl.pallas_call(finish, out_shape=[jax.ShapeDtypeStruct(phase.shape, jnp.f...]
where the time goes in v2:
time: 37.7 us; the launch traced here: 37.5 us
  Pallas kernels  36.9 us (98%)
  between operations  0.64 us (2%)
    pallas_call x1, Pallas kernels, per_device(): pl.pallas_call(functools.partial(kernel, ngx, ngy), out_shape=[jax.ShapeD...  35.7 us
    pallas_call x1, Pallas kernels, per_device(): pl.pallas_call(finish, out_shape=[jax.ShapeDtypeStruct(phase.shape, jnp.f...  1.2 us

profile of v2, /device:TPU:1, one launch (start us, length us, event | category | flops | bytes accessed | tf_op | source)
XLA Modules:
  0.0 37.5 jit_solution(7049724341491496649)
XLA Ops:
  0.6 35.7 %shard_map.85 = (f32[8,8,256]{2,1,0:T(8,128)S(1)}, f32[8,8,256]{2,1,0:T(8,128)S(1)}, f32[19,10,32,128]{3,2,1,0:T(8,128)S(1)}) custom-call(f32[16]{0:T(128)} %angle_in.1, f32[8,8,256]{2,1,0:T(8,128)} %phase_in.1, f32[8,8,256]{2,1,0:T(8,128)} %solute_in.1, s32[8,8,256]{2,1,0:T(8,128)} %grain_in.1, s32[8,16]{1,0:T(8,128)} %flags_in.1, f32[19,8,16,128]{3,2,1,0:T(8,128)} %pops.1), custom_call_target="tpu_custom_call" | custom-call | tf_op jit(solution)/shard_map/pallas_call | solution.py:290
  36.3 1.2 %shard_map.86 = (f32[8,8,256]{2,1,0:T(8,128)}, f32[8,8,256]{2,1,0:T(8,128)}, f32[19,8,16,128]{3,2,1,0:T(8,128)}) custom-call(f32[8,8,256]{2,1,0:T(8,128)S(1)} %get-tuple-element.6.phase_next, f32[8,8,256]{2,1,0:T(8,128)S(1)} %get-tuple-element.7.solute_next, f32[19,10,32,128]{3,2,1,0:T(8,128)S(1)} %get-tuple-element.8.s2), custom_call_target="tpu_custom_call" | custom-call | tf_op jit(solution)/shard_map/pallas_call | solution.py:329

commit v3 on v2

--- a/solution.py
+++ b/solution.py
@@ -36,6 +36,7 @@
 ORDER = YP + YM + (0, 1, 2, 5, 6, 11, 12, 13, 14)
 SLOT = tuple(ORDER.index(comp) for comp in range(19))
 EDGES = ((15, 1, 1), (16, -1, -1), (17, -1, 1), (18, 1, -1))
+OPPOSITE = (0, 2, 1, 4, 3, 6, 5, 8, 7, 10, 9, 12, 11, 14, 13, 16, 15, 18, 17)
 BODY_FORCE = 0.01
 GRAINS = 16
 
@@ -54,7 +55,7 @@
     return values
 
 
-def collide(g, solid):
+def relax(g):
     dif = {i: g[i] - g[i + 1] for i in range(1, 19, 2)}
     add = {i: g[i] + g[i + 1] for i in range(1, 19, 2)}
     axes = add[1] + add[3] + add[5]
@@ -82,19 +83,36 @@
         15: uy + uz,
         17: uy - uz,
     }
-    posts = [None] * 19
-    relaxed = base - 0.25 * g[0]
-    posts[0] = relaxed + solid * (g[0] - relaxed)
+    relaxed = [None] * 19
+    relaxed[0] = base - 0.25 * g[0]
     for i, a in along.items():
         even = base + square * (a * a)
         odd = linear * a
         if VELOCITY[i][0]:
             odd = odd + 3.0 * BODY_FORCE
-        plus = even + odd - 0.25 * g[i]
-        minus = even - odd - 0.25 * g[i + 1]
-        posts[i] = plus + solid * (g[i + 1] - plus)
-        posts[i + 1] = minus + solid * (g[i] - minus)
-    return posts
+        relaxed[i] = even + odd - 0.25 * g[i]
+        relaxed[i + 1] = even - odd - 0.25 * g[i + 1]
+    return relaxed
+
+
+def blend(relaxed, back, solid):
+    return relaxed + solid * (back - relaxed)
+
+
+def next_phase(ph, lap, dx, dy, so, cos_cell, sin_cell):
+    gx, gy = 0.5 * dx, 0.5 * dy
+    sx, sy = gx * gx, gy * gy
+    denom = sx + sy + 0.25
+    inv = 1.0 / (denom * denom)
+    cos_four = (sx * sx - 6.0 * sx * sy + sy * sy) * inv
+    sin_four = 4.0 * gx * gy * (sx - sy) * inv
+    aniso = 1.0 + 0.3 * (cos_four * cos_cell + sin_four * sin_cell)
+    bulk = 1.0 - ph * ph
+    return ph + 0.08 * aniso * aniso * (lap + ph - ph * ph * ph - 1.5 * so * bulk * bulk)
+
+
+def solid_of(ph):
+    return jnp.clip(0.5 * (1.0 + ph), 0.0, 1.0)
 
 
 def streamed(buf, comp, y):
@@ -109,8 +127,10 @@
     ngx, ngy,
     angle_in, phase_in, solute_in, grain_in, flags_in, pops,
     phase_out, solute_out, s2,
-    angle, phase, solute, grain, flags, pv, ysend, yrecv, xrecv, tsend, trecv, solid_p, s1, zsend, zrecv, csend, crecv,
-    in_sem, fs_sem, fr_sem, ts_sem, tr_sem, ls_sem, lr_sem,
+    angle, phase, solute, grain, flags, pv, rel, ysend, yrecv, xrecv, dsend, drecv,
+    tsend, trecv, solid_p, closed, solid_z, solid_h, s1,
+    yab, yab_in, zab, zab_in, cab, cab_in, zsend, zrecv, csend, crecv,
+    in_sem, fs_sem, fr_sem, bs_sem, br_sem, ts_sem, tr_sem, ls_sem, lr_sem,
 ):
     me_x, me_y = lax.axis_index("gx"), lax.axis_index("gy")
 
@@ -137,18 +157,62 @@
         pl.semaphore_signal(barrier, inc=1, device_id=device, device_id_type=MESH)
     loads[0].wait()
     loads[1].wait()
-    for field, ref in enumerate((phase, solute)):
-        ysend[0, field] = ref[:, 7, :]
-        ysend[1, field] = ref[:, 0, :]
+    loads[3].wait()
+    for side, edge, second in ((0, 7, 6), (1, 0, 1)):
+        ysend[side, 0] = phase[:, edge, :]
+        ysend[side, 1] = phase[:, second, :]
+        ysend[side, 2] = solute[:, edge, :]
+        ysend[side, 3] = grain[:, edge, :].astype(jnp.float32)
+    for n, (_, dx, dy) in enumerate(EDGES):
+        line = phase[7 if dx > 0 else 0, 7 if dy > 0 else 0 : 8 if dy > 0 else 1, :]
+        dsend[n, 0:1] = line[:, :128]
+        dsend[n, 1:2] = line[:, 128:]
     pl.semaphore_wait(barrier, len(partners))
 
     faces = []
-    for side, step in ((0, 1), (1, -1)):
-        faces.append(remote(ysend.at[side], yrecv.at[side], fs_sem.at[side], fr_sem.at[side], dev(0, step)))
+    for n, (_, dx, dy) in enumerate(EDGES):
+        faces.append(remote(dsend.at[n], drecv.at[n], fs_sem.at[6 + n], fr_sem.at[6 + n], dev(dx, dy)))
     for side, step, layer in ((0, 1, 7), (1, -1, 0)):
         for field, ref in enumerate((phase, solute)):
             n = 2 + 2 * side + field
             faces.append(remote(ref.at[layer], xrecv.at[side, field], fs_sem.at[n], fr_sem.at[n], dev(step, 0)))
+    for side, step in ((0, 1), (1, -1)):
+        faces.append(remote(ysend.at[side], yrecv.at[side], fs_sem.at[side], fr_sem.at[side], dev(0, step)))
+
+    loads[4].wait()
+    open_row = jnp.concatenate([flags[y : y + 1, :] for y in range(8)], axis=1)
+    first = lax.broadcasted_iota(jnp.int32, (128, 128), 0) == 0
+    closed[...] = jnp.transpose(jnp.where(first & (open_row == 0), 1.0, 0.0)).reshape(8, 16, 128)
+
+    loads[5].wait()
+
+    def first_relax(y, carry):
+        g = [pv[comp, y] for comp in range(19)]
+        shut = closed[y] > 0.5
+        for comp, value in enumerate(relax(g)):
+            rel[comp, y] = jnp.where(shut, g[OPPOSITE[comp]], value)
+        return carry
+
+    lax.fori_loop(0, 8, first_relax, 0)
+    early = []
+    for side, comps, z, dx in ((0, ZP, 15, 1), (1, ZM, 0, -1)):
+        for n, comp in enumerate(comps):
+            zab[side, 0, n] = rel[comp, :, z, :]
+            zab[side, 1, n] = pv[OPPOSITE[comp], :, z, :]
+        early.append(remote(zab.at[side], zab_in.at[side], bs_sem.at[side], br_sem.at[side], dev(dx, 0)))
+    for n, (comp, dx, dy) in enumerate(EDGES):
+        y, z = (7 if dy > 0 else 0), (15 if dx > 0 else 0)
+        cab[n, 0:1] = rel[comp, y, z : z + 1, :]
+        cab[n, 1:2] = pv[OPPOSITE[comp], y, z : z + 1, :]
+        early.append(remote(cab.at[n], cab_in.at[n], bs_sem.at[4 + n], br_sem.at[4 + n], dev(dx, dy)))
+    for side, comps, y in ((0, YP, 7), (1, YM, 0)):
+        for n, comp in enumerate(comps):
+            yab[side, 0, n] = rel[comp, y]
+            yab[side, 1, n] = pv[OPPOSITE[comp], y]
+    for copy in faces:
+        copy.wait_send()
+    for side, step in ((0, 1), (1, -1)):
+        early.append(remote(yab.at[side], yab_in.at[side], bs_sem.at[2 + side], br_sem.at[2 + side], dev(0, step)))
 
     loads[2].wait()
     lane = lax.broadcasted_iota(jnp.int32, (8, 128), 1)
@@ -158,21 +222,16 @@
     cos_table, sin_table = jnp.cos(4.0 * table), jnp.sin(4.0 * table)
     cos_of = [jnp.broadcast_to(cos_table[:, i : i + 1], (8, 256)) for i in range(GRAINS)]
     sin_of = [jnp.broadcast_to(sin_table[:, i : i + 1], (8, 256)) for i in range(GRAINS)]
-    cos_cell, sin_cell = [], []
-    loads[3].wait()
-    for x in range(8):
-        ids = grain[x]
+
+    def trig(ids):
         c, s = cos_of, sin_of
         for bit in (1, 2, 4, 8):
             on = (ids & bit) != 0
             c = [jnp.where(on, c[2 * i + 1], c[2 * i]) for i in range(len(c) // 2)]
             s = [jnp.where(on, s[2 * i + 1], s[2 * i]) for i in range(len(s) // 2)]
-        cos_cell.append(c[0])
-        sin_cell.append(s[0])
-
-    loads[4].wait()
-    open_row = jnp.concatenate([flags[y : y + 1, :] for y in range(8)], axis=1)
-
+        return c[0], s[0]
+
+    cells = [trig(grain[x]) for x in range(8)]
     for copy in faces:
         copy.wait_recv()
     row = lax.broadcasted_iota(jnp.int32, (8, 256), 0)
@@ -181,8 +240,8 @@
         value = ref[x]
         xplus = ref[x + 1] if x < 7 else xrecv[1, field]
         xminus = ref[x - 1] if x > 0 else xrecv[0, field]
-        yplus = jnp.where(row == 7, yrecv[1, field, x : x + 1, :], pltpu.roll(value, 7, 0))
-        yminus = jnp.where(row == 0, yrecv[0, field, x : x + 1, :], pltpu.roll(value, 1, 0))
+        yplus = jnp.where(row == 7, yrecv[1, 2 * field, x : x + 1, :], pltpu.roll(value, 7, 0))
+        yminus = jnp.where(row == 0, yrecv[0, 2 * field, x : x + 1, :], pltpu.roll(value, 1, 0))
         zplus, zminus = pltpu.roll(value, 255, 1), pltpu.roll(value, 1, 1)
         laplace = (xplus + xminus) + (yplus + yminus) + (zplus + zminus) - 6.0 * value
         return value, laplace, xplus - xminus, yplus - yminus
@@ -191,25 +250,37 @@
     for x in range(8):
         ph, lap, dx, dy = around(phase, 0, x)
         so, lap_so, _, _ = around(solute, 1, x)
-        gx, gy = 0.5 * dx, 0.5 * dy
-        sx, sy = gx * gx, gy * gy
-        denom = sx + sy + 0.25
-        inv = 1.0 / (denom * denom)
-        cos_four = (sx * sx - 6.0 * sx * sy + sy * sy) * inv
-        sin_four = 4.0 * gx * gy * (sx - sy) * inv
-        aniso = 1.0 + 0.3 * (cos_four * cos_cell[x] + sin_four * sin_cell[x])
-        bulk = 1.0 - ph * ph
-        change = 0.08 * aniso * aniso * (lap + ph - ph * ph * ph - 1.5 * so * bulk * bulk)
-        ph_next = ph + change
+        ph_next = next_phase(ph, lap, dx, dy, so, *cells[x])
         phase_out[x] = ph_next
         solute_out[x] = so + 0.16 * lap_so + 0.5 * (ph_next - ph)
-        solids.append(jnp.clip(0.5 * (1.0 + ph_next), 0.0, 1.0))
+        solids.append(solid_of(ph_next))
+
+    beyond = []
+    for side in range(2):
+        ph, second, so, ids = (yrecv[side, n] for n in range(4))
+        inner = ysend[1 - side, 0]
+        yplus, yminus = (inner, second) if side == 0 else (second, inner)
+        lines = {}
+        for n, (_, dx, dy) in enumerate(EDGES):
+            if dy == (1 if side == 0 else -1):
+                lines[dx] = jnp.concatenate([drecv[n, 0:1], drecv[n, 1:2]], axis=1)
+        xplus = jnp.where(row == 7, lines[-1], pltpu.roll(ph, 7, 0))
+        xminus = jnp.where(row == 0, lines[1], pltpu.roll(ph, 1, 0))
+        lap = (xplus + xminus) + (yplus + yminus) + (pltpu.roll(ph, 255, 1) + pltpu.roll(ph, 1, 1)) - 6.0 * ph
+        ph_next = next_phase(ph, lap, xplus - xminus, yplus - yminus, so, *trig(ids.astype(jnp.int32)))
+        beyond.append(solid_of(ph_next))
 
     rows = swap_groups(solids, 0, 1)
+    tiles = []
     for half in range(2):
-        tiles = swap_groups([r[:, 128 * half : 128 * half + 128] for r in rows], 1, 16)
-        for j in range(8):
-            tsend[8 * half + j] = tiles[j]
+        tiles += swap_groups([r[:, 128 * half : 128 * half + 128] for r in rows], 1, 16)
+    last_lane = (lane & 15) == 15
+    for k in range(ngx):
+        tsend[k, 0] = tiles[k]
+        tsend[k, 1] = jnp.where(last_lane, tiles[k - 1], tiles[(k + 1) % ngx])
+        below = pltpu.roll(beyond[0], (272 - 16 * k) % 256, 1)[:, :128]
+        above = pltpu.roll(beyond[1], (336 - 16 * k) % 256, 1)[:, :128]
+        tsend[k, 2] = jnp.where(lane < 64, below, above)
     moves = []
     for d in range(1, ngx):
         device = dev(d, 0)
@@ -217,25 +288,46 @@
             remote(tsend.at[device["gx"]], trecv.at[me_x], ts_sem.at[d - 1], tr_sem.at[d - 1], device)
         )
     trecv[me_x] = tsend[me_x]
-    loads[5].wait()
     for copy in moves:
         copy.wait_recv()
-    whole = trecv[...].reshape(128, 128)
-    first = lax.broadcasted_iota(jnp.int32, (128, 128), 0) == 0
-    whole = jnp.where(first & (open_row == 0), 1.0, whole)
-    solid_p[...] = jnp.transpose(whole).reshape(8, 16, 128)
+    solid_p[...] = jnp.maximum(jnp.transpose(trecv[:, 0].reshape(128, 128)).reshape(8, 16, 128), closed[...])
+    solid_z[...] = jnp.transpose(trecv[:, 1].reshape(128, 128)).reshape(8, 16, 128)
+    solid_h[...] = jnp.transpose(trecv[:, 2].reshape(128, 128))
+
+    def first_step(y, carry):
+        solid = solid_p[y]
+        for comp in range(19):
+            s1[SLOT[comp], y + 1, 8:24, :] = blend(rel[comp, y], pv[OPPOSITE[comp], y], solid)
+        return carry
+
+    lax.fori_loop(0, 8, first_step, 0)
+    for copy in early:
+        copy.wait_recv()
+    for side, comps, z, lane_z in ((0, ZP, 7, 15), (1, ZM, 24, 0)):
+        solid = solid_z[:, lane_z, :]
+        for n, comp in enumerate(comps):
+            s1[SLOT[comp], 1:9, z, :] = blend(zab_in[side, 0, n], zab_in[side, 1, n], solid)
+    for side, comps, y in ((0, YP, 0), (1, YM, 9)):
+        solid = solid_h[64 * side + 16 : 64 * side + 32, :]
+        for n, comp in enumerate(comps):
+            s1[SLOT[comp], y, 8:24, :] = blend(yab_in[side, 0, n], yab_in[side, 1, n], solid)
+    for n, (comp, dx, dy) in enumerate(EDGES):
+        y, z = (0 if dy > 0 else 9), (7 if dx > 0 else 24)
+        at = (0 if dy > 0 else 64) + (15 if dx > 0 else 32)
+        s1[SLOT[comp], y, z : z + 1, :] = blend(cab_in[n, 0:1], cab_in[n, 1:2], solid_h[at : at + 1, :])
 
     pending = []
 
-    def step(which, buf, source):
+    def step(buf):
         def one(t, carry):
             y = lax.rem(t + 7, 8)
-            posts = collide(source(y), solid_p[y])
-            for comp in range(19):
-                buf[SLOT[comp], y + 1, 8:24, :] = posts[comp]
+            g = [streamed(s1, comp, y) for comp in range(19)]
+            solid = solid_p[y]
+            for comp, value in enumerate(relax(g)):
+                buf[SLOT[comp], y + 1, 8:24, :] = blend(value, g[OPPOSITE[comp]], solid)
             return carry
 
-        sems = lambda n: (ls_sem.at[which, n], lr_sem.at[which, n])
+        sems = lambda n: (ls_sem.at[n], lr_sem.at[n])
         lax.fori_loop(0, 2, one, 0)
         copies = [
             remote(buf.at[0:5, 8, 8:24], buf.at[0:5, 0, 8:24], *sems(0), dev(0, 1)),
@@ -243,27 +335,25 @@
         ]
         for n, (comp, dx, dy) in enumerate(EDGES):
             y, z = (8 if dy > 0 else 1), (23 if dx > 0 else 8)
-            csend[which, n, 0:1] = buf[SLOT[comp], y, z : z + 1, :]
-            copies.append(remote(csend.at[which, n], crecv.at[which, n], *sems(2 + n), dev(dx, dy)))
+            csend[n, 0:1] = buf[SLOT[comp], y, z : z + 1, :]
+            copies.append(remote(csend.at[n], crecv.at[n], *sems(2 + n), dev(dx, dy)))
         lax.fori_loop(2, 8, one, 0)
         for side, comps, z, dx in ((0, ZP, 23, 1), (1, ZM, 8, -1)):
             for n, comp in enumerate(comps):
-                zsend[which, side, n] = buf[SLOT[comp], 1:9, z, :]
-            copies.append(remote(zsend.at[which, side], zrecv.at[which, side], *sems(6 + side), dev(dx, 0)))
+                zsend[side, n] = buf[SLOT[comp], 1:9, z, :]
+            copies.append(remote(zsend.at[side], zrecv.at[side], *sems(6 + side), dev(dx, 0)))
         for copy in copies:
             copy.wait_recv()
         pending.extend(copies)
         for side, comps, z in ((0, ZP, 7), (1, ZM, 24)):
             for n, comp in enumerate(comps):
-                buf[SLOT[comp], 1:9, z, :] = zrecv[which, side, n]
+                buf[SLOT[comp], 1:9, z, :] = zrecv[side, n]
         for n, (comp, dx, dy) in enumerate(EDGES):
             y, z = (0 if dy > 0 else 9), (7 if dx > 0 else 24)
-            buf[SLOT[comp], y, z : z + 1, :] = crecv[which, n, 0:1]
-
-    step(0, s1, lambda y: [pv[comp, y] for comp in range(19)])
-    step(1, s2, lambda y: [streamed(s1, comp, y) for comp in range(19)])
-
-    for copy in faces + moves + pending:
+            buf[SLOT[comp], y, z : z + 1, :] = crecv[n, 0:1]
+
+    step(s2)
+    for copy in early + moves + pending:
         copy.wait_send()
 
 
@@ -303,24 +393,38 @@
             pltpu.VMEM((8, 8, 256), jnp.int32),
             pltpu.VMEM((8, 16), jnp.int32),
             pltpu.VMEM((19, 8, 16, 128), jnp.float32),
+            pltpu.VMEM((19, 8, 16, 128), jnp.float32),
+            pltpu.VMEM((2, 4, 8, 256), jnp.float32),
+            pltpu.VMEM((2, 4, 8, 256), jnp.float32),
             pltpu.VMEM((2, 2, 8, 256), jnp.float32),
-            pltpu.VMEM((2, 2, 8, 256), jnp.float32),
-            pltpu.VMEM((2, 2, 8, 256), jnp.float32),
-            pltpu.VMEM((ngx, 8, 128), jnp.float32),
-            pltpu.VMEM((ngx, 8, 128), jnp.float32),
+            pltpu.VMEM((4, 8, 128), jnp.float32),
+            pltpu.VMEM((4, 8, 128), jnp.float32),
+            pltpu.VMEM((ngx, 3, 8, 128), jnp.float32),
+            pltpu.VMEM((ngx, 3, 8, 128), jnp.float32),
             pltpu.VMEM((8, 16, 128), jnp.float32),
+            pltpu.VMEM((8, 16, 128), jnp.float32),
+            pltpu.VMEM((8, 16, 128), jnp.float32),
+            pltpu.VMEM((128, 128), jnp.float32),
             pltpu.VMEM((19, 10, 32, 128), jnp.float32),
+            pltpu.VMEM((2, 2, 5, 16, 128), jnp.float32),
+            pltpu.VMEM((2, 2, 5, 16, 128), jnp.float32),
             pltpu.VMEM((2, 2, 5, 8, 128), jnp.float32),
             pltpu.VMEM((2, 2, 5, 8, 128), jnp.float32),
-            pltpu.VMEM((2, 4, 8, 128), jnp.float32),
-            pltpu.VMEM((2, 4, 8, 128), jnp.float32),
+            pltpu.VMEM((4, 8, 128), jnp.float32),
+            pltpu.VMEM((4, 8, 128), jnp.float32),
+            pltpu.VMEM((2, 5, 8, 128), jnp.float32),
+            pltpu.VMEM((2, 5, 8, 128), jnp.float32),
+            pltpu.VMEM((4, 8, 128), jnp.float32),
+            pltpu.VMEM((4, 8, 128), jnp.float32),
             pltpu.SemaphoreType.DMA((6,)),
-            pltpu.SemaphoreType.DMA((6,)),
-            pltpu.SemaphoreType.DMA((6,)),
+            pltpu.SemaphoreType.DMA((10,)),
+            pltpu.SemaphoreType.DMA((10,)),
+            pltpu.SemaphoreType.DMA((8,)),
+            pltpu.SemaphoreType.DMA((8,)),
             pltpu.SemaphoreType.DMA((ngx - 1,)),
             pltpu.SemaphoreType.DMA((ngx - 1,)),
-            pltpu.SemaphoreType.DMA((2, 8)),
-            pltpu.SemaphoreType.DMA((2, 8)),
+            pltpu.SemaphoreType.DMA((8,)),
+            pltpu.SemaphoreType.DMA((8,)),
         ],
         compiler_params=pltpu.CompilerParams(
             collective_id=0, has_side_effects=True, vmem_limit_bytes=40 * 1024 * 1024

time: 37.7 us -> 33.6 us (0.89)
  Pallas kernels: 36.9 us -> 32.8 us
    pallas_call x1, Pallas kernels: 35.7 us -> 31.6 us  [per_device(): pl.pallas_call(functools.partial(kernel, ngx, ngy), out_shape=[jax.ShapeD...]
where the time goes in v3:
time: 33.6 us; the launch traced here: 33.4 us
  Pallas kernels  32.8 us (98%)
  between operations  0.64 us (2%)
    pallas_call x1, Pallas kernels, per_device(): pl.pallas_call(functools.partial(kernel, ngx, ngy), out_shape=[jax.ShapeD...  31.6 us
    pallas_call x1, Pallas kernels, per_device(): pl.pallas_call(finish, out_shape=[jax.ShapeDtypeStruct(phase.shape, jnp.f...  1.2 us

profile of v3, /device:TPU:1, one launch (start us, length us, event | category | flops | bytes accessed | tf_op | source)
XLA Modules:
  0.0 33.4 jit_solution(12274758196281192437)
XLA Ops:
  0.6 31.6 %shard_map.85 = (f32[8,8,256]{2,1,0:T(8,128)S(1)}, f32[8,8,256]{2,1,0:T(8,128)S(1)}, f32[19,10,32,128]{3,2,1,0:T(8,128)S(1)}) custom-call(f32[16]{0:T(128)} %angle_in.1, f32[8,8,256]{2,1,0:T(8,128)} %phase_in.1, f32[8,8,256]{2,1,0:T(8,128)} %solute_in.1, s32[8,8,256]{2,1,0:T(8,128)} %grain_in.1, s32[8,16]{1,0:T(8,128)} %flags_in.1, f32[19,8,16,128]{3,2,1,0:T(8,128)} %pops.1), custom_call_target="tpu_custom_call" | custom-call | tf_op jit(solution)/shard_map/pallas_call | solution.py:380
  32.2 1.2 %shard_map.86 = (f32[8,8,256]{2,1,0:T(8,128)}, f32[8,8,256]{2,1,0:T(8,128)}, f32[19,8,16,128]{3,2,1,0:T(8,128)}) custom-call(f32[8,8,256]{2,1,0:T(8,128)S(1)} %get-tuple-element.6.phase_next, f32[8,8,256]{2,1,0:T(8,128)S(1)} %get-tuple-element.7.solute_next, f32[19,10,32,128]{3,2,1,0:T(8,128)S(1)} %get-tuple-element.8.s2), custom_call_target="tpu_custom_call" | custom-call | tf_op jit(solution)/shard_map/pallas_call | solution.py:433

commit v4 on v3

--- a/solution.py
+++ b/solution.py
@@ -144,17 +144,18 @@
         copy.start()
         return copy
 
+    far_first = sorted(range(1, ngx), key=lambda d: (abs(d % 8 - 4), abs(d - 8)))
+    partners = [dev(dx, dy) for _, dx, dy in EDGES]
+    partners += [dev(d, 0) for d in far_first] + [dev(0, 1), dev(0, -1)]
+    barrier = pltpu.get_barrier_semaphore()
+    for device in partners:
+        pl.semaphore_signal(barrier, inc=1, device_id=device, device_id_type=MESH)
     loads = []
     for n, (src, dst) in enumerate(
         ((phase_in, phase), (solute_in, solute), (angle_in, angle), (grain_in, grain), (flags_in, flags), (pops, pv))
     ):
         loads.append(pltpu.make_async_copy(src, dst, in_sem.at[n]))
         loads[-1].start()
-    partners = [dev(d, 0) for d in range(1, ngx)] + [dev(0, 1), dev(0, -1)]
-    partners += [dev(dx, dy) for _, dx, dy in EDGES]
-    barrier = pltpu.get_barrier_semaphore()
-    for device in partners:
-        pl.semaphore_signal(barrier, inc=1, device_id=device, device_id_type=MESH)
     loads[0].wait()
     loads[1].wait()
     loads[3].wait()
@@ -186,15 +187,25 @@
 
     loads[5].wait()
 
-    def first_relax(y, carry):
+    def first_relax(t, carry):
+        y = lax.rem(t + 7, 8)
         g = [pv[comp, y] for comp in range(19)]
         shut = closed[y] > 0.5
         for comp, value in enumerate(relax(g)):
             rel[comp, y] = jnp.where(shut, g[OPPOSITE[comp]], value)
         return carry
 
-    lax.fori_loop(0, 8, first_relax, 0)
+    lax.fori_loop(0, 2, first_relax, 0, unroll=2)
     early = []
+    for side, comps, y in ((0, YP, 7), (1, YM, 0)):
+        for n, comp in enumerate(comps):
+            yab[side, 0, n] = rel[comp, y]
+            yab[side, 1, n] = pv[OPPOSITE[comp], y]
+    for copy in faces:
+        copy.wait_send()
+    for side, step in ((0, 1), (1, -1)):
+        early.append(remote(yab.at[side], yab_in.at[side], bs_sem.at[2 + side], br_sem.at[2 + side], dev(0, step)))
+    lax.fori_loop(2, 8, first_relax, 0, unroll=2)
     for side, comps, z, dx in ((0, ZP, 15, 1), (1, ZM, 0, -1)):
         for n, comp in enumerate(comps):
             zab[side, 0, n] = rel[comp, :, z, :]
@@ -205,14 +216,6 @@
         cab[n, 0:1] = rel[comp, y, z : z + 1, :]
         cab[n, 1:2] = pv[OPPOSITE[comp], y, z : z + 1, :]
         early.append(remote(cab.at[n], cab_in.at[n], bs_sem.at[4 + n], br_sem.at[4 + n], dev(dx, dy)))
-    for side, comps, y in ((0, YP, 7), (1, YM, 0)):
-        for n, comp in enumerate(comps):
-            yab[side, 0, n] = rel[comp, y]
-            yab[side, 1, n] = pv[OPPOSITE[comp], y]
-    for copy in faces:
-        copy.wait_send()
-    for side, step in ((0, 1), (1, -1)):
-        early.append(remote(yab.at[side], yab_in.at[side], bs_sem.at[2 + side], br_sem.at[2 + side], dev(0, step)))
 
     loads[2].wait()
     lane = lax.broadcasted_iota(jnp.int32, (8, 128), 1)
@@ -249,10 +252,8 @@
     solids = []
     for x in range(8):
         ph, lap, dx, dy = around(phase, 0, x)
-        so, lap_so, _, _ = around(solute, 1, x)
-        ph_next = next_phase(ph, lap, dx, dy, so, *cells[x])
+        ph_next = next_phase(ph, lap, dx, dy, solute[x], *cells[x])
         phase_out[x] = ph_next
-        solute_out[x] = so + 0.16 * lap_so + 0.5 * (ph_next - ph)
         solids.append(solid_of(ph_next))
 
     beyond = []
@@ -282,12 +283,15 @@
         above = pltpu.roll(beyond[1], (336 - 16 * k) % 256, 1)[:, :128]
         tsend[k, 2] = jnp.where(lane < 64, below, above)
     moves = []
-    for d in range(1, ngx):
+    for d in far_first:
         device = dev(d, 0)
         moves.append(
             remote(tsend.at[device["gx"]], trecv.at[me_x], ts_sem.at[d - 1], tr_sem.at[d - 1], device)
         )
     trecv[me_x] = tsend[me_x]
+    for x in range(8):
+        so, lap_so, _, _ = around(solute, 1, x)
+        solute_out[x] = so + 0.16 * lap_so + 0.5 * (phase_out[x] - phase[x])
     for copy in moves:
         copy.wait_recv()
     solid_p[...] = jnp.maximum(jnp.transpose(trecv[:, 0].reshape(128, 128)).reshape(8, 16, 128), closed[...])
@@ -300,7 +304,8 @@
             s1[SLOT[comp], y + 1, 8:24, :] = blend(rel[comp, y], pv[OPPOSITE[comp], y], solid)
         return carry
 
-    lax.fori_loop(0, 8, first_step, 0)
+    for y in (0, 1, 6, 7):
+        first_step(y, 0)
     for copy in early:
         copy.wait_recv()
     for side, comps, z, lane_z in ((0, ZP, 7, 15), (1, ZM, 24, 0)):
@@ -328,16 +333,18 @@
             return carry
 
         sems = lambda n: (ls_sem.at[n], lr_sem.at[n])
-        lax.fori_loop(0, 2, one, 0)
-        copies = [
-            remote(buf.at[0:5, 8, 8:24], buf.at[0:5, 0, 8:24], *sems(0), dev(0, 1)),
-            remote(buf.at[5:10, 1, 8:24], buf.at[5:10, 9, 8:24], *sems(1), dev(0, -1)),
-        ]
+        lax.fori_loop(0, 2, one, 0, unroll=2)
+        copies = []
         for n, (comp, dx, dy) in enumerate(EDGES):
             y, z = (8 if dy > 0 else 1), (23 if dx > 0 else 8)
             csend[n, 0:1] = buf[SLOT[comp], y, z : z + 1, :]
             copies.append(remote(csend.at[n], crecv.at[n], *sems(2 + n), dev(dx, dy)))
-        lax.fori_loop(2, 8, one, 0)
+        copies += [
+            remote(buf.at[0:5, 8, 8:24], buf.at[0:5, 0, 8:24], *sems(0), dev(0, 1)),
+            remote(buf.at[5:10, 1, 8:24], buf.at[5:10, 9, 8:24], *sems(1), dev(0, -1)),
+        ]
+        lax.fori_loop(2, 6, first_step, 0, unroll=2)
+        lax.fori_loop(2, 8, one, 0, unroll=2)
         for side, comps, z, dx in ((0, ZP, 23, 1), (1, ZM, 8, -1)):
             for n, comp in enumerate(comps):
                 zsend[side, n] = buf[SLOT[comp], 1:9, z, :]

time: 33.6 us -> 33.1 us (0.985)
  Pallas kernels: 32.8 us -> 32.3 us
    pallas_call x1, Pallas kernels: 31.6 us -> 31.1 us  [per_device(): pl.pallas_call(functools.partial(kernel, ngx, ngy), out_shape=[jax.ShapeD...]
where the time goes in v4:
time: 33.1 us; the launch traced here: 33 us
  Pallas kernels  32.3 us (98%)
  between operations  0.64 us (2%)
    pallas_call x1, Pallas kernels, per_device(): pl.pallas_call(functools.partial(kernel, ngx, ngy), out_shape=[jax.ShapeD...  31.1 us
    pallas_call x1, Pallas kernels, per_device(): pl.pallas_call(finish, out_shape=[jax.ShapeDtypeStruct(phase.shape, jnp.f...  1.2 us

profile of v4, /device:TPU:1, one launch (start us, length us, event | category | flops | bytes accessed | tf_op | source)
XLA Modules:
  0.0 33.0 jit_solution(10454209774289116848)
XLA Ops:
  0.6 31.1 %shard_map.85 = (f32[8,8,256]{2,1,0:T(8,128)S(1)}, f32[8,8,256]{2,1,0:T(8,128)S(1)}, f32[19,10,32,128]{3,2,1,0:T(8,128)S(1)}) custom-call(f32[16]{0:T(128)} %angle_in.1, f32[8,8,256]{2,1,0:T(8,128)} %phase_in.1, f32[8,8,256]{2,1,0:T(8,128)} %solute_in.1, s32[8,8,256]{2,1,0:T(8,128)} %grain_in.1, s32[8,16]{1,0:T(8,128)} %flags_in.1, f32[19,8,16,128]{3,2,1,0:T(8,128)} %pops.1), custom_call_target="tpu_custom_call" | custom-call | tf_op jit(solution)/shard_map/pallas_call | solution.py:387
  31.8 1.2 %shard_map.86 = (f32[8,8,256]{2,1,0:T(8,128)}, f32[8,8,256]{2,1,0:T(8,128)}, f32[19,8,16,128]{3,2,1,0:T(8,128)}) custom-call(f32[8,8,256]{2,1,0:T(8,128)S(1)} %get-tuple-element.6.phase_next, f32[8,8,256]{2,1,0:T(8,128)S(1)} %get-tuple-element.7.solute_next, f32[19,10,32,128]{3,2,1,0:T(8,128)S(1)} %get-tuple-element.8.s2), custom_call_target="tpu_custom_call" | custom-call | tf_op jit(solution)/shard_map/pallas_call | solution.py:440

commit v5 on v4

--- a/solution.py
+++ b/solution.py
@@ -126,9 +126,9 @@
 def kernel(
     ngx, ngy,
     angle_in, phase_in, solute_in, grain_in, flags_in, pops,
-    phase_out, solute_out, s2,
+    phase_out, solute_out, out,
     angle, phase, solute, grain, flags, pv, rel, ysend, yrecv, xrecv, dsend, drecv,
-    tsend, trecv, solid_p, closed, solid_z, solid_h, s1,
+    tsend, trecv, solid_p, closed, solid_z, solid_h, s1, s2,
     yab, yab_in, zab, zab_in, cab, cab_in, zsend, zrecv, csend, crecv,
     in_sem, fs_sem, fr_sem, bs_sem, br_sem, ts_sem, tr_sem, ls_sem, lr_sem,
 ):
@@ -201,7 +201,7 @@
         for n, comp in enumerate(comps):
             yab[side, 0, n] = rel[comp, y]
             yab[side, 1, n] = pv[OPPOSITE[comp], y]
-    for copy in faces:
+    for copy in faces[8:]:
         copy.wait_send()
     for side, step in ((0, 1), (1, -1)):
         early.append(remote(yab.at[side], yab_in.at[side], bs_sem.at[2 + side], br_sem.at[2 + side], dev(0, step)))
@@ -349,33 +349,48 @@
             for n, comp in enumerate(comps):
                 zsend[side, n] = buf[SLOT[comp], 1:9, z, :]
             copies.append(remote(zsend.at[side], zrecv.at[side], *sems(6 + side), dev(dx, 0)))
+        def inner(y, carry):
+            for comp in range(19):
+                out[comp, y] = streamed(buf, comp, y)
+            return carry
+
+        lax.fori_loop(1, 7, inner, 0, unroll=2)
+        for comp in range(19):
+            if VELOCITY[comp][1] <= 0:
+                out[comp, 0] = streamed(buf, comp, 0)
+            if VELOCITY[comp][1] >= 0:
+                out[comp, 7] = streamed(buf, comp, 7)
         for copy in copies:
             copy.wait_recv()
         pending.extend(copies)
-        for side, comps, z in ((0, ZP, 7), (1, ZM, 24)):
+        for side, comps, z in ((0, ZP, 0), (1, ZM, 15)):
             for n, comp in enumerate(comps):
-                buf[SLOT[comp], 1:9, z, :] = zrecv[side, n]
+                vx, vy, _ = VELOCITY[comp]
+                value = zrecv[side, n]
+                if vx:
+                    value = pltpu.roll(value, vx % 128, 1)
+                out[comp, max(vy, 0) : 8 + min(vy, 0), z, :] = value[max(-vy, 0) : 8 - max(vy, 0)]
         for n, (comp, dx, dy) in enumerate(EDGES):
             y, z = (0 if dy > 0 else 9), (7 if dx > 0 else 24)
             buf[SLOT[comp], y, z : z + 1, :] = crecv[n, 0:1]
+        for comps, y in ((YP, 0), (YM, 7)):
+            for comp in comps:
+                out[comp, y] = streamed(buf, comp, y)
 
     step(s2)
-    for copy in early + moves + pending:
+    for copy in faces[:8] + early + moves + pending:
         copy.wait_send()
 
 
-def finish(phase_next, solute_next, s2, phase_out, solute_out, out, buf, sems):
-    copies = [
-        pltpu.make_async_copy(phase_next, phase_out, sems.at[8]),
-        pltpu.make_async_copy(solute_next, solute_out, sems.at[9]),
-    ]
+def finish(*refs):
+    sems = refs[-1]
+    phase_next, solute_next, pops_next, phase_out, solute_out, out = refs[:-1]
+    pairs = [(phase_next, phase_out), (solute_next, solute_out)]
+    pairs += [(pops_next.at[c : c + 5], out.at[c : c + 5]) for c in (0, 5, 10)]
+    pairs += [(pops_next.at[15:19], out.at[15:19])]
+    copies = [pltpu.make_async_copy(src, dst, sems.at[n]) for n, (src, dst) in enumerate(pairs)]
     for copy in copies:
         copy.start()
-    for y in range(8):
-        for comp in range(19):
-            buf[comp, y] = streamed(s2, comp, y)
-        copies.append(pltpu.make_async_copy(buf.at[:, y], out.at[:, y], sems.at[y]))
-        copies[-1].start()
     for copy in copies:
         copy.wait()
 
@@ -384,12 +399,12 @@
     vmem = pl.BlockSpec(memory_space=pltpu.VMEM)
     operands = (grain_angle, phase, solute, grain, inlet_flags, populations)
     hbm = pl.BlockSpec(memory_space=pltpu.HBM)
-    phase_next, solute_next, s2 = pl.pallas_call(
+    phase_next, solute_next, pops_next = pl.pallas_call(
         functools.partial(kernel, ngx, ngy),
         out_shape=[
             jax.ShapeDtypeStruct(phase.shape, jnp.float32),
             jax.ShapeDtypeStruct(solute.shape, jnp.float32),
-            jax.ShapeDtypeStruct((19, 10, 32, 128), jnp.float32),
+            jax.ShapeDtypeStruct(populations.shape, jnp.float32),
         ],
         in_specs=[hbm] * 6,
         out_specs=[vmem, vmem, vmem],
@@ -412,6 +427,7 @@
             pltpu.VMEM((8, 16, 128), jnp.float32),
             pltpu.VMEM((8, 16, 128), jnp.float32),
             pltpu.VMEM((128, 128), jnp.float32),
+            pltpu.VMEM((19, 10, 32, 128), jnp.float32),
             pltpu.VMEM((19, 10, 32, 128), jnp.float32),
             pltpu.VMEM((2, 2, 5, 16, 128), jnp.float32),
             pltpu.VMEM((2, 2, 5, 16, 128), jnp.float32),
@@ -446,9 +462,9 @@
         ],
         in_specs=[vmem] * 3,
         out_specs=[hbm] * 3,
-        scratch_shapes=[pltpu.VMEM((19, 8, 16, 128), jnp.float32), pltpu.SemaphoreType.DMA((10,))],
+        scratch_shapes=[pltpu.SemaphoreType.DMA((6,))],
         compiler_params=pltpu.CompilerParams(vmem_limit_bytes=40 * 1024 * 1024),
-    )(phase_next, solute_next, s2)
+    )(phase_next, solute_next, pops_next)
 
 
 def solution(mesh):

time: 33.1 us -> 33.1 us (level)
  no operation moved by 1% of the time
where the time goes in v5:
time: 33.1 us; the launch traced here: 32.9 us
  Pallas kernels  32.3 us (98%)
  between operations  0.64 us (2%)
    pallas_call x1, Pallas kernels, per_device(): pl.pallas_call(functools.partial(kernel, ngx, ngy), out_shape=[jax.ShapeD...  31.2 us
    pallas_call x1, Pallas kernels, per_device(): pl.pallas_call(finish, out_shape=[jax.ShapeDtypeStruct(phase.shape, jnp.f...  1.12 us

profile of v5, /device:TPU:1, one launch (start us, length us, event | category | flops | bytes accessed | tf_op | source)
XLA Modules:
  0.0 32.9 jit_solution(10549672962444440338)
XLA Ops:
  0.6 31.2 %shard_map.85 = (f32[8,8,256]{2,1,0:T(8,128)S(1)}, f32[8,8,256]{2,1,0:T(8,128)S(1)}, f32[19,8,16,128]{3,2,1,0:T(8,128)S(1)}) custom-call(f32[16]{0:T(128)} %angle_in.1, f32[8,8,256]{2,1,0:T(8,128)} %phase_in.1, f32[8,8,256]{2,1,0:T(8,128)} %solute_in.1, s32[8,8,256]{2,1,0:T(8,128)} %grain_in.1, s32[8,16]{1,0:T(8,128)} %flags_in.1, f32[19,8,16,128]{3,2,1,0:T(8,128)} %pops.1), custom_call_target="tpu_custom_call" | custom-call | tf_op jit(solution)/shard_map/pallas_call | solution.py:402
  31.8 1.1 %shard_map.86 = (f32[8,8,256]{2,1,0:T(8,128)}, f32[8,8,256]{2,1,0:T(8,128)}, f32[19,8,16,128]{3,2,1,0:T(8,128)}) custom-call(f32[8,8,256]{2,1,0:T(8,128)S(1)} %get-tuple-element.6.refs_0_, f32[8,8,256]{2,1,0:T(8,128)S(1)} %get-tuple-element.7.refs_1_, f32[19,8,16,128]{3,2,1,0:T(8,128)S(1)} %get-tuple-element.8.refs_2_), custom_call_target="tpu_custom_call" | custom-call | tf_op jit(solution)/shard_map/pallas_call | solution.py:456
